TPU v7x, 256 devices: a whole 4x4x8 slice. The times are simulated.
256 devices in a mesh: row: 16 (over z_hi, x, core), col: 16 (over z_lo, y).
Axes of the slice: x: 4, y: 4, z: 8 (z_hi: 2, z_lo: 4; z = z_hi * 4 + z_lo), core: 2. Of those that a mesh axis runs over, the one named last changes fastest.
Arguments:
- upper_vals: bfloat16 [512, 6, 128, 128], P(('row', 'col')), may hold values from -1 to 1
- upper_cols: int32 [512, 6], P(('row', 'col')), may hold values from 0 to 511, as said below
- result_cols: int32 [512, 8], P(('row', 'col')), may hold values from 0 to 511, as said below
Outputs:
- result_blocks: bfloat16 [512, 8, 128, 128], P(('row', 'col'))
Inputs may be any that keep to these rules, and one draw needn't show every extreme that they name: `upper_cols`: slot 0 of block row I holds I; its other slots hold 5 distinct columns (I + k) mod 512 with 1 <= k <= 7. `result_cols`: block row I holds 8 distinct columns (I + k) mod 512 with 1 <= k <= 14.
All inputs are finite; a program needn't handle non-finite values.
Results may differ from a plain program's by a relative error of at most 0.0035.
Values may be sent and summed in bfloat16 or wider, within the bound.
A program may use at most 64 MiB of HBM per device.

v0:
```python
import jax
import jax.numpy as jnp
from jax import lax
from jax.sharding import PartitionSpec as P

W = 7


def for_sending(array):

    def short(part):
        return part.astype(jnp.bfloat16) if part.dtype == jnp.float32 else part

    return jax.tree.map(short, array)


def passed_along(block, axis, distance):
    devices = range(lax.axis_size(axis))
    route = [((i - distance) % len(devices), i) for i in devices]
    return lax.ppermute(block, axis, route)


def band_rows(upper_win, offset_win, band_reach):
    row_total = upper_win.shape[0] - band_reach
    select = (
        offset_win[:, :, None] == jnp.arange(band_reach + 1, dtype=jnp.int32)[None, None, :]
    ).astype(jnp.bfloat16)
    packed = jnp.einsum(
        "nso,nsab->noab", select, upper_win, preferred_element_type=jnp.float32
    ).astype(jnp.bfloat16)
    own_rows = packed[band_reach:]
    diagonal = own_rows[:, 0].astype(jnp.float32)
    diagonal = (diagonal + jnp.swapaxes(diagonal, -1, -2)).astype(jnp.bfloat16)
    lower_part = [
        jnp.swapaxes(
            packed[band_reach - shift_by : band_reach - shift_by + row_total, shift_by], -1, -2
        )
        for shift_by in range(band_reach, 0, -1)
    ]
    return jnp.concatenate(
        [jnp.stack(lower_part, axis=1), diagonal[:, None], own_rows[:, 1:]], axis=1
    )


def select_kept(every_step, step_all):
    picked = jnp.take_along_axis(every_step, (step_all - 1)[:, :, None, None], axis=1)
    return picked.astype(jnp.bfloat16)


def dense_products(band_window, row_count, band_reach):
    band_width = 2 * band_reach + 1
    own_band = band_window[:row_count]
    every_step = []
    for step in range(1, 2 * band_reach + 1):
        own_part = own_band[:, step:]
        partner = band_window[step : step + row_count, : band_width - step]
        every_step.append(
            jnp.einsum("reac,rebc->rab", own_part, partner, preferred_element_type=jnp.float32)
        )
    return jnp.stack(every_step, axis=1)


def fetch_behind(payload, needed):
    row_count = payload[0].shape[0]
    hop_count = (needed + row_count - 1) // row_count
    received = []
    for distance in range(hop_count, 0, -1):
        keep_rows = min(row_count, needed - (distance - 1) * row_count)
        segment = tuple((member[row_count - keep_rows :] for member in payload))
        received.append(
            jax.tree.map(
                lambda part, own: part.astype(own.dtype),
                passed_along(for_sending(segment), ("row", "col"), distance),
                segment,
            )
        )
    return tuple(
        (
            jnp.concatenate([arrived[member_index] for arrived in received], axis=0)
            for member_index in range(len(payload))
        )
    )


def fetch_ahead(payload, needed):
    row_count = payload[0].shape[0]
    hop_count = (needed + row_count - 1) // row_count
    received = []
    for distance in range(1, hop_count + 1):
        keep_rows = min(row_count, needed - (distance - 1) * row_count)
        segment = tuple((member for member in payload))
        received.append(
            jax.tree.map(
                lambda part, own: part.astype(own.dtype),
                passed_along(for_sending(segment), ("row", "col"), -distance),
                segment,
            )
        )
    return tuple(
        (
            jnp.concatenate([arrived[member_index] for arrived in received], axis=0)
            for member_index in range(len(payload))
        )
    )


def on_device(upper_vals, upper_cols, result_cols):
    row_count = upper_vals.shape[0]
    band_reach = W
    block_total = row_count * lax.axis_size("row") * lax.axis_size("col")
    first_row = (lax.axis_index("row") * lax.axis_size("col") + lax.axis_index("col")) * row_count
    local_ids = first_row + jnp.arange(row_count, dtype=jnp.int32)
    offsets = (upper_cols - local_ids[:, None]) % block_total
    step_all = (result_cols - local_ids[:, None]) % block_total
    behind_vals, behind_offsets = fetch_behind((upper_vals, offsets), band_reach)
    own_band = band_rows(
        jnp.concatenate([behind_vals, upper_vals], axis=0),
        jnp.concatenate([behind_offsets, offsets], axis=0),
        band_reach,
    )
    (ahead_band,) = fetch_ahead((own_band,), 2 * band_reach)
    band_window = jnp.concatenate([own_band, ahead_band], axis=0)
    every_step = dense_products(band_window, row_count, band_reach)
    return select_kept(every_step, step_all)


def solution(mesh):
    in_specs = (
        P(("row", "col"), None, None, None),
        P(("row", "col"), None),
        P(("row", "col"), None),
    )
    out_specs = P(("row", "col"), None, None, None)
    return jax.shard_map(
        on_device, mesh=mesh, in_specs=in_specs, out_specs=out_specs, check_vma=False
    )
```

profile of v0, /device:TPU:235, one launch (start us, length us, event | category | flops | bytes accessed | tf_op | source)
XLA Modules:
  0.0 348.2 jit_solution(2928814061240258957)
XLA Ops:
  0.0 1.3 copy.193
  1.3 3.1 collective-permute-start.5
  4.4 2.3 collective-permute-start.6
  6.7 1.9 collective-permute-start.7
  8.6 1.4 collective-permute-start.4
  10.0 0.8 and_select_fusion
  10.8 1.1 collective-permute-start
  11.9 9.0 %collective-permute-done = s32[1,6]{1,0:T(1,128)S(1)} collective-permute-done((s32[1,6]{1,0:T(1,128)S(1)}, s32[1,6]{1,0:T(1,128)S(1)}, u32[]{:S(2)}, u32[]{:S(2)}) %collective-permute-start) | collective-permute-done | bytes 56 | tf_op jit(solution)/shard_map/ppermute | solution.py:20
  20.9 12.8 %collective-permute-done.1 = s32[2,6]{1,0:T(2,128)S(1)} collective-permute-done((s32[2,6]{1,0:T(2,128)S(1)}, s32[2,6]{1,0:T(2,128)S(1)}, u32[]{:S(2)}, u32[]{:S(2)}) %collective-permute-start.1) | collective-permute-done | bytes 80 | tf_op jit(solution)/shard_map/ppermute | solution.py:20
  33.7 15.6 %collective-permute-start.2 = (s32[2,6]{1,0:T(2,128)S(1)}, s32[2,6]{1,0:T(2,128)S(1)}, u32[]{:S(2)}, u32[]{:S(2)}) collective-permute-start(s32[2,6]{1,0:T(2,128)S(1)} %and_select_fusion), channel_id=1, source_target_pairs={{254,0},{255,1},{0,2},{1,3},{2,4},{3,5},{4,6},{5,7},{6,8},{7,9},{8... | collective-permute-start | bytes 152 | tf_op jit(solution)/shard_map/ppermute | solution.py:20
  49.3 0.7 collective-permute-done.2
  50.0 4.9 %collective-permute-start.3 = (s32[2,6]{1,0:T(2,128)S(1)}, s32[2,6]{1,0:T(2,128)S(1)}, u32[]{:S(2)}, u32[]{:S(2)}) collective-permute-start(s32[2,6]{1,0:T(2,128)S(1)} %and_select_fusion), channel_id=1, source_target_pairs={{255,0},{0,1},{1,2},{2,3},{3,4},{4,5},{5,6},{6,7},{7,8},{8,9},{9,1... | collective-permute-start | bytes 152 | tf_op jit(solution)/shard_map/ppermute | solution.py:20
  55.0 0.7 collective-permute-done.3
  56.1 0.3 constant_dynamic-update-slice_fusion
  56.4 0.8 convolution_convert_fusion
  57.2 1.8 fusion.55
  59.2 0.6 copy.330
  59.8 1.6 copy.213
  61.4 1.6 copy.290
  63.1 1.6 copy.205
  64.7 1.6 copy.291
  66.3 1.6 copy.206
  67.9 0.7 copy.292
  68.7 0.9 copy.207
  69.6 0.7 copy.293
  70.3 0.9 copy.208
  71.3 0.7 copy.294
  72.0 0.9 copy.209
  73.0 0.7 copy.295
  73.7 0.9 copy.210
  74.7 0.8 copy.204
  75.4 0.9 fusion.41
  76.5 5.1 %concatenate.57 = bf16[2,15,128,128]{3,1,2,0:T(8,128)(2,1)} concatenate(bf16[2,1,128,128]{3,1,2,0:T(2,128)(2,1)} %copy.213, bf16[2,1,128,128]{3,1,2,0:T(2,128)(2,1)} %copy.205, bf16[2,1,128,128]{3,1,2,0:T(2,128)(2,1)} %copy.206, bf16[2,1,128,128]{3,1,2,0:T(2,128)(2,1)S(1)} %copy.207, bf16[2,1,128,128]{3,1,2,0:T(2,128)(2,1)S(1)} %copy.208, bf16[2,1,128,128]{3,1,2,0:T(2,128)(2,1)S(1)} %copy.209, ...), dimensions={1} | concatenate | bytes 1966080 | tf_op jit(solution)/shard_map/concatenate | solution.py:40
  81.6 2.5 copy.221
  84.1 0.9 collective-permute-start.8
  85.2 12.7 %concatenate.56 = bf16[2,14,128,128]{3,1,2,0:T(8,128)(2,1)} concatenate(bf16[2,1,128,128]{3,1,2,0:T(2,128)(2,1)} %copy.205, bf16[2,1,128,128]{3,1,2,0:T(2,128)(2,1)} %copy.206, bf16[2,1,128,128]{3,1,2,0:T(2,128)(2,1)S(1)} %copy.207, bf16[2,1,128,128]{3,1,2,0:T(2,128)(2,1)S(1)} %copy.208, bf16[2,1,128,128]{3,1,2,0:T(2,128)(2,1)S(1)} %copy.209, ...), dimensions={1} | concatenate | bytes 1835008 | tf_op jit(solution)/shard_map/concatenate | solution.py:40
  97.9 12.6 %concatenate.59 = bf16[2,13,128,128]{3,1,2,0:T(8,128)(2,1)} concatenate(bf16[2,1,128,128]{3,1,2,0:T(2,128)(2,1)} %copy.206, bf16[2,1,128,128]{3,1,2,0:T(2,128)(2,1)S(1)} %copy.207, bf16[2,1,128,128]{3,1,2,0:T(2,128)(2,1)S(1)} %copy.208, bf16[2,1,128,128]{3,1,2,0:T(2,128)(2,1)S(1)} %copy.209, bf16[2,1,128,128]{3,1,2,0:T(2,128)(2,1)S(1)} %copy.210, ...), dimensions={1} | concatenate | bytes 1703936 | tf_op jit(solution)/shard_map/concatenate | solution.py:40
  110.5 11.3 %concatenate.60 = bf16[2,12,128,128]{3,1,2,0:T(8,128)(2,1)} concatenate(bf16[2,1,128,128]{3,1,2,0:T(2,128)(2,1)S(1)} %copy.207, bf16[2,1,128,128]{3,1,2,0:T(2,128)(2,1)S(1)} %copy.208, bf16[2,1,128,128]{3,1,2,0:T(2,128)(2,1)S(1)} %copy.209, bf16[2,1,128,128]{3,1,2,0:T(2,128)(2,1)S(1)} %copy.210, bf16[2,1,128,128]{3,1,2,0:T(2,128)(2,1)S(1)} %copy.211, ...), dimensions={1} | concatenate | bytes 1572864 | tf_op jit(solution)/shard_map/concatenate | solution.py:40
  121.8 11.1 %concatenate.62 = bf16[2,11,128,128]{3,1,2,0:T(8,128)(2,1)} concatenate(bf16[2,1,128,128]{3,1,2,0:T(2,128)(2,1)S(1)} %copy.208, bf16[2,1,128,128]{3,1,2,0:T(2,128)(2,1)S(1)} %copy.209, bf16[2,1,128,128]{3,1,2,0:T(2,128)(2,1)S(1)} %copy.210, bf16[2,1,128,128]{3,1,2,0:T(2,128)(2,1)S(1)} %copy.211, bf16[2,7,128,128]{3,1,2,0:T(8,128)(2,1)S(1)} %slice.164), dimensions={1} | concatenate | bytes 1441792 | tf_op jit(solution)/shard_map/concatenate | solution.py:40
  133.0 1.5 collective-permute-start.10
  134.5 2.9 collective-permute-start.11
  137.7 4.9 %collective-permute-start.12 = (bf16[2,15,128,128]{3,2,1,0:T(8,128)(2,1)}, bf16[2,15,128,128]{3,2,1,0:T(8,128)(2,1)S(1)}, u32[]{:S(2)}, u32[]{:S(2)}) collective-permute-start(bf16[2,15,128,128]{3,2,1,0:T(8,128)(2,1)} %copy.221), channel_id=1, source_target_pairs={{5,0},{6,1},{7,2},{8,3},{9,4},{10,5},{11,6},{12,7},{13,8},{14,9},{... | collective-permute-start | bytes 2949128 | tf_op jit(solution)/shard_map/ppermute | solution.py:20
  143.3 0.9 pad_maximum_fusion.1
  144.3 0.7 pad_maximum_fusion.2
  145.0 7.2 %collective-permute-start.13 = (bf16[2,15,128,128]{3,2,1,0:T(8,128)(2,1)}, bf16[2,15,128,128]{3,2,1,0:T(8,128)(2,1)S(1)}, u32[]{:S(2)}, u32[]{:S(2)}) collective-permute-start(bf16[2,15,128,128]{3,2,1,0:T(8,128)(2,1)} %copy.221), channel_id=1, source_target_pairs={{6,0},{7,1},{8,2},{9,3},{10,4},{11,5},{12,6},{13,7},{14,8},{15,9},... | collective-permute-start | bytes 2949128 | tf_op jit(solution)/shard_map/ppermute | solution.py:20
  152.2 1.8 copy.222
  154.3 0.4 fusion.13
  154.7 0.6 copy-done.4
  155.3 1.7 fusion.12
  156.9 3.4 collective-permute-start.14
  160.3 1.5 fusion.11
  161.8 1.5 fusion.10
  163.3 5.9 %collective-permute-done.10 = bf16[2,15,128,128]{3,2,1,0:T(8,128)(2,1)S(1)} collective-permute-done((bf16[2,15,128,128]{3,2,1,0:T(8,128)(2,1)}, bf16[2,15,128,128]{3,2,1,0:T(8,128)(2,1)S(1)}, u32[]{:S(2)}, u32[]{:S(2)}) %collective-permute-start.10) | collective-permute-done | bytes 983072 | tf_op jit(solution)/shard_map/ppermute | solution.py:20
  169.3 1.3 fusion.9
  170.6 0.4 fusion.8
  171.0 20.8 %collective-permute-done.11 = bf16[2,15,128,128]{3,2,1,0:T(8,128)(2,1)S(1)} collective-permute-done((bf16[2,15,128,128]{3,2,1,0:T(8,128)(2,1)}, bf16[2,15,128,128]{3,2,1,0:T(8,128)(2,1)S(1)}, u32[]{:S(2)}, u32[]{:S(2)}) %collective-permute-start.11) | collective-permute-done | bytes 983072 | tf_op jit(solution)/shard_map/ppermute | solution.py:20
  191.8 0.3 fusion.5
  192.1 0.3 fusion.4
  192.4 29.7 %collective-permute-done.12 = bf16[2,15,128,128]{3,2,1,0:T(8,128)(2,1)S(1)} collective-permute-done((bf16[2,15,128,128]{3,2,1,0:T(8,128)(2,1)}, bf16[2,15,128,128]{3,2,1,0:T(8,128)(2,1)S(1)}, u32[]{:S(2)}, u32[]{:S(2)}) %collective-permute-start.12) | collective-permute-done | bytes 983072 | tf_op jit(solution)/shard_map/ppermute | solution.py:20
  222.4 0.3 fusion.2
  222.7 1.3 collective-permute-done.13
  224.6 121.6 %collective-permute-done.14 = bf16[2,15,128,128]{3,2,1,0:T(8,128)(2,1)S(1)} collective-permute-done((bf16[2,15,128,128]{3,2,1,0:T(8,128)(2,1)}, bf16[2,15,128,128]{3,2,1,0:T(8,128)(2,1)S(1)}, u32[]{:S(2)}, u32[]{:S(2)}) %collective-permute-start.14) | collective-permute-done | bytes 983072 | tf_op jit(solution)/shard_map/ppermute | solution.py:20
  346.5 0.7 gather_fusion
  347.2 1.0 select_convert_fusion
  (48 shorter events, 3.1 us)
Async XLA Ops:
  0.0 56.1 %copy-start.2 = (bf16[2,6,128,128]{3,2,1,0:T(8,128)(2,1)S(1)}, bf16[2,6,128,128]{3,2,1,0:T(8,128)(2,1)}, u32[]{:S(2)}) copy-start(bf16[2,6,128,128]{3,2,1,0:T(8,128)(2,1)} %param.3) | copy-start | bytes 1179652
  1.3 54.5 %collective-permute-start.5 = (bf16[2,6,128,128]{3,1,2,0:T(8,128)(2,1)S(1)}, bf16[2,6,128,128]{3,1,2,0:T(8,128)(2,1)S(1)}, u32[]{:S(2)}, u32[]{:S(2)}) collective-permute-start(bf16[2,6,128,128]{3,1,2,0:T(8,128)(2,1)S(1)} %copy.193), channel_id=1, source_target_pairs={{253,0},{254,1},{255,2},{0,3},{1,4},{2,5},{3,6},{4,7},{5,8},{6,9},... | collective-permute-start | bytes 1179656 | tf_op jit(solution)/shard_map/ppermute | solution.py:20
  4.4 51.5 %collective-permute-start.6 = (bf16[2,6,128,128]{3,1,2,0:T(8,128)(2,1)S(1)}, bf16[2,6,128,128]{3,1,2,0:T(8,128)(2,1)S(1)}, u32[]{:S(2)}, u32[]{:S(2)}) collective-permute-start(bf16[2,6,128,128]{3,1,2,0:T(8,128)(2,1)S(1)} %copy.193), channel_id=1, source_target_pairs={{254,0},{255,1},{0,2},{1,3},{2,4},{3,5},{4,6},{5,7},{6,8},{7,9},{8... | collective-permute-start | bytes 1179656 | tf_op jit(solution)/shard_map/ppermute | solution.py:20
  6.7 49.3 %collective-permute-start.7 = (bf16[2,6,128,128]{3,1,2,0:T(8,128)(2,1)S(1)}, bf16[2,6,128,128]{3,1,2,0:T(8,128)(2,1)S(1)}, u32[]{:S(2)}, u32[]{:S(2)}) collective-permute-start(bf16[2,6,128,128]{3,1,2,0:T(8,128)(2,1)S(1)} %copy.193), channel_id=1, source_target_pairs={{255,0},{0,1},{1,2},{2,3},{3,4},{4,5},{5,6},{6,7},{7,8},{8,9},{9,1... | collective-permute-start | bytes 1179656 | tf_op jit(solution)/shard_map/ppermute | solution.py:20
  8.6 47.2 %collective-permute-start.4 = (bf16[1,6,128,128]{3,1,2,0:T(8,128)(2,1)S(1)}, bf16[1,6,128,128]{3,1,2,0:T(8,128)(2,1)S(1)}, u32[]{:S(2)}, u32[]{:S(2)}) collective-permute-start(bf16[1,6,128,128]{3,1,2,0:T(8,128)(2,1)S(1)} %slice.156), channel_id=1, source_target_pairs={{252,0},{253,1},{254,2},{255,3},{0,4},{1,5},{2,6},{3,7},{4,8},{5,9... | collective-permute-start | bytes 589832 | tf_op jit(solution)/shard_map/ppermute | solution.py:20
  10.8 10.1 %collective-permute-start = (s32[1,6]{1,0:T(1,128)S(1)}, s32[1,6]{1,0:T(1,128)S(1)}, u32[]{:S(2)}, u32[]{:S(2)}) collective-permute-start(s32[1,6]{1,0:T(1,128)S(1)} %slice.123), channel_id=1, source_target_pairs={{252,0},{253,1},{254,2},{255,3},{0,4},{1,5},{2,6},{3,7},{4,8},{5,9... | collective-permute-start | bytes 80 | tf_op jit(solution)/shard_map/ppermute | solution.py:20
  20.9 12.8 %collective-permute-start.1 = (s32[2,6]{1,0:T(2,128)S(1)}, s32[2,6]{1,0:T(2,128)S(1)}, u32[]{:S(2)}, u32[]{:S(2)}) collective-permute-start(s32[2,6]{1,0:T(2,128)S(1)} %and_select_fusion), channel_id=1, source_target_pairs={{253,0},{254,1},{255,2},{0,3},{1,4},{2,5},{3,6},{4,7},{5,8},{6,9},... | collective-permute-start | bytes 152 | tf_op jit(solution)/shard_map/ppermute | solution.py:20
  33.7 16.4 %collective-permute-start.2 = (s32[2,6]{1,0:T(2,128)S(1)}, s32[2,6]{1,0:T(2,128)S(1)}, u32[]{:S(2)}, u32[]{:S(2)}) collective-permute-start(s32[2,6]{1,0:T(2,128)S(1)} %and_select_fusion), channel_id=1, source_target_pairs={{254,0},{255,1},{0,2},{1,3},{2,4},{3,5},{4,6},{5,7},{6,8},{7,9},{8... | collective-permute-start | bytes 152 | tf_op jit(solution)/shard_map/ppermute | solution.py:20
  50.0 5.7 %collective-permute-start.3 = (s32[2,6]{1,0:T(2,128)S(1)}, s32[2,6]{1,0:T(2,128)S(1)}, u32[]{:S(2)}, u32[]{:S(2)}) collective-permute-start(s32[2,6]{1,0:T(2,128)S(1)} %and_select_fusion), channel_id=1, source_target_pairs={{255,0},{0,1},{1,2},{2,3},{3,4},{4,5},{5,6},{6,7},{7,8},{8,9},{9,1... | collective-permute-start | bytes 152 | tf_op jit(solution)/shard_map/ppermute | solution.py:20
  76.4 8.6 %copy-start.7 = (s32[2,8]{1,0:T(2,128)S(1)}, s32[2,8]{1,0:T(2,128)}, u32[]{:S(2)}) copy-start(s32[2,8]{1,0:T(2,128)} %param.5) | copy-start | bytes 196
  84.1 60.9 %collective-permute-start.8 = (bf16[2,15,128,128]{3,2,1,0:T(8,128)(2,1)}, bf16[2,15,128,128]{3,2,1,0:T(8,128)(2,1)}, u32[]{:S(2)}, u32[]{:S(2)}) collective-permute-start(bf16[2,15,128,128]{3,2,1,0:T(8,128)(2,1)} %copy.221), channel_id=1, source_target_pairs={{1,0},{2,1},{3,2},{4,3},{5,4},{6,5},{7,6},{8,7},{9,8},{10,9},{11,1... | collective-permute-start | bytes 2949128 | tf_op jit(solution)/shard_map/ppermute | solution.py:20
  110.5 46.4 %collective-permute-start.9 = (bf16[2,15,128,128]{3,2,1,0:T(8,128)(2,1)}, bf16[2,15,128,128]{3,2,1,0:T(8,128)(2,1)}, u32[]{:S(2)}, u32[]{:S(2)}) collective-permute-start(bf16[2,15,128,128]{3,2,1,0:T(8,128)(2,1)} %copy.221), channel_id=1, source_target_pairs={{2,0},{3,1},{4,2},{5,3},{6,4},{7,5},{8,6},{9,7},{10,8},{11,9},{12,... | collective-permute-start | bytes 2949128 | tf_op jit(solution)/shard_map/ppermute | solution.py:20
  133.0 36.3 %collective-permute-start.10 = (bf16[2,15,128,128]{3,2,1,0:T(8,128)(2,1)}, bf16[2,15,128,128]{3,2,1,0:T(8,128)(2,1)S(1)}, u32[]{:S(2)}, u32[]{:S(2)}) collective-permute-start(bf16[2,15,128,128]{3,2,1,0:T(8,128)(2,1)} %copy.221), channel_id=1, source_target_pairs={{3,0},{4,1},{5,2},{6,3},{7,4},{8,5},{9,6},{10,7},{11,8},{12,9},{13... | collective-permute-start | bytes 2949128 | tf_op jit(solution)/shard_map/ppermute | solution.py:20
  134.5 57.3 %collective-permute-start.11 = (bf16[2,15,128,128]{3,2,1,0:T(8,128)(2,1)}, bf16[2,15,128,128]{3,2,1,0:T(8,128)(2,1)S(1)}, u32[]{:S(2)}, u32[]{:S(2)}) collective-permute-start(bf16[2,15,128,128]{3,2,1,0:T(8,128)(2,1)} %copy.221), channel_id=1, source_target_pairs={{4,0},{5,1},{6,2},{7,3},{8,4},{9,5},{10,6},{11,7},{12,8},{13,9},{1... | collective-permute-start | bytes 2949128 | tf_op jit(solution)/shard_map/ppermute | solution.py:20
  137.7 84.5 %collective-permute-start.12 = (bf16[2,15,128,128]{3,2,1,0:T(8,128)(2,1)}, bf16[2,15,128,128]{3,2,1,0:T(8,128)(2,1)S(1)}, u32[]{:S(2)}, u32[]{:S(2)}) collective-permute-start(bf16[2,15,128,128]{3,2,1,0:T(8,128)(2,1)} %copy.221), channel_id=1, source_target_pairs={{5,0},{6,1},{7,2},{8,3},{9,4},{10,5},{11,6},{12,7},{13,8},{14,9},{... | collective-permute-start | bytes 2949128 | tf_op jit(solution)/shard_map/ppermute | solution.py:20
  144.3 9.8 %copy-start = (bf16[2,15,128,128]{3,1,2,0:T(8,128)(2,1)S(1)}, bf16[2,15,128,128]{3,1,2,0:T(8,128)(2,1)}, u32[]{:S(2)}) copy-start(bf16[2,15,128,128]{3,1,2,0:T(8,128)(2,1)} %concatenate.57) | copy-start | bytes 2949124
  144.9 9.3 %copy-start.5 = (bf16[2,14,128,128]{3,1,2,0:T(8,128)(2,1)S(1)}, bf16[2,14,128,128]{3,1,2,0:T(8,128)(2,1)}, u32[]{:S(2)}) copy-start(bf16[2,14,128,128]{3,1,2,0:T(8,128)(2,1)} %concatenate.56) | copy-start | bytes 2752516
  145.0 79.1 %collective-permute-start.13 = (bf16[2,15,128,128]{3,2,1,0:T(8,128)(2,1)}, bf16[2,15,128,128]{3,2,1,0:T(8,128)(2,1)S(1)}, u32[]{:S(2)}, u32[]{:S(2)}) collective-permute-start(bf16[2,15,128,128]{3,2,1,0:T(8,128)(2,1)} %copy.221), channel_id=1, source_target_pairs={{6,0},{7,1},{8,2},{9,3},{10,4},{11,5},{12,6},{13,7},{14,8},{15,9},... | collective-permute-start | bytes 2949128 | tf_op jit(solution)/shard_map/ppermute | solution.py:20
  154.0 1.2 copy-start.4
  154.3 6.0 %copy-start.1 = (bf16[2,12,128,128]{3,1,2,0:T(8,128)(2,1)S(1)}, bf16[2,12,128,128]{3,1,2,0:T(8,128)(2,1)}, u32[]{:S(2)}) copy-start(bf16[2,12,128,128]{3,1,2,0:T(8,128)(2,1)} %concatenate.60) | copy-start | bytes 2359300
  155.3 6.6 %copy-start.3 = (bf16[2,11,128,128]{3,1,2,0:T(8,128)(2,1)S(1)}, bf16[2,11,128,128]{3,1,2,0:T(8,128)(2,1)}, u32[]{:S(2)}) copy-start(bf16[2,11,128,128]{3,1,2,0:T(8,128)(2,1)} %concatenate.62) | copy-start | bytes 2162692
  156.9 189.2 %collective-permute-start.14 = (bf16[2,15,128,128]{3,2,1,0:T(8,128)(2,1)}, bf16[2,15,128,128]{3,2,1,0:T(8,128)(2,1)S(1)}, u32[]{:S(2)}, u32[]{:S(2)}) collective-permute-start(bf16[2,15,128,128]{3,2,1,0:T(8,128)(2,1)} %copy.221), channel_id=1, source_target_pairs={{7,0},{8,1},{9,2},{10,3},{11,4},{12,5},{13,6},{14,7},{15,8},{16,9}... | collective-permute-start | bytes 2949128 | tf_op jit(solution)/shard_map/ppermute | solution.py:20
  222.7 123.6 %copy-start.6 = (bf16[2,1,128,128]{3,1,2,0:T(2,128)(2,1)S(1)}, bf16[2,1,128,128]{3,1,2,0:T(2,128)(2,1)}, u32[]{:S(2)}) copy-start(bf16[2,1,128,128]{3,1,2,0:T(2,128)(2,1)} %get-tuple-element.7) | copy-start | bytes 196612
where the time goes:
time: 352 us; the launch traced here: 348 us
  waiting for transfers between devices  203 us (58%)
  local copies, waits for them, and re-layouts  77.7 us (22%)
  starting transfers between devices  51.2 us (15%)
  matrix products  9.64 us (3%)
  other arithmetic  6.6 us (2%)
    ppermute x15, waiting for transfers between devices, passed_along(): return lax.ppermute(block, axis, route)  203 us
    concatenate x6, local copies, waits for them, and re-layouts, band_rows(): jnp.concatenate([jnp.stack(lower_part, axis=1), diagonal[:, None], own_ro...  55.4 us
    ppermute x15, starting transfers between devices, passed_along(): return lax.ppermute(block, axis, route)  51.2 us
    dot_general x14, matrix products, dense_products(): jnp.einsum('reac,rebc->rab', own_part, partner, preferred_element_type=jn...  8.88 us
    another operation x7, local copies, waits for them, and re-layouts, band_rows(): jnp.stack(lower_part, axis=1)  8.58 us
  transfers between devices with their start and end apart: 15, of which 9 were waited for; matrix products, arithmetic and copies ran while one was open for 18% of the time, Pallas kernels for 0%

commit v1 on v0

v1 whole, which is shorter than its diff:
```python
import jax
import jax.numpy as jnp
from jax import lax
from jax.experimental import pallas as pl
from jax.experimental.pallas import tpu as pltpu
from jax.sharding import PartitionSpec as P

BLK = 128
REACH = 7
SLOTS = 6
NONE = SLOTS
ROWS = 2
STEPS = 2 * REACH
FIRST = REACH - 1
LAST = 2 * REACH
BEHIND = (-3, -2, -1)
AHEAD = (1, 2, 3, 4)
OTHERS = BEHIND + AHEAD
SENT = {
    -3: ((0, 2), (1, 3)),
    -2: ((0, 4), (1, 5)),
    -1: ((0, 5), (1, 5)),
    1: ((0, 6), (1, 6)),
    2: ((0, 6), (1, 6)),
    3: ((0, 6), (1, 6)),
    4: ((0, 6),),
}


def band_kernel(device_total, block_total, vals, cols, kept, out, *scratch):
    held = dict(zip(OTHERS, scratch[:7]))
    places = dict(zip(OTHERS, scratch[7:14]))
    own, own_places, left, right, every, send_sem, recv_sem, psend_sem, precv_sem = scratch[14:]
    inner = lax.axis_size("col")
    me = lax.axis_index("row") * inner + lax.axis_index("col")

    def device(distance):
        there = lax.rem(me + distance + device_total, device_total)
        return (there // inner, lax.rem(there, inner))

    barrier = pltpu.get_barrier_semaphore()
    for m in (-4, -3, -2, -1, 1, 2, 3, 4):
        pl.semaphore_signal(barrier, inc=1, device_id=device(m), device_id_type=pl.DeviceIdType.MESH)

    zero = jnp.zeros((BLK, BLK), jnp.bfloat16)
    for r in range(ROWS):
        offs = [lax.rem(cols[r, s] - (me * ROWS + r) + block_total, block_total) for s in range(SLOTS)]
        ranks = [
            sum((offs[t] > offs[s]).astype(jnp.int32) for t in range(1, SLOTS) if t != s)
            for s in range(1, SLOTS)
        ]
        for j in range(SLOTS - 1):
            slot = sum(s * (ranks[s - 1] == j).astype(jnp.int32) for s in range(1, SLOTS))
            own[r, j] = vals[r, jnp.minimum(slot, SLOTS - 1)]
        own[r, SLOTS - 1] = vals[r, 0]
        own[r, NONE] = zero
        own_places[r, 0] = SLOTS - 1
        for o in range(1, REACH + 1):
            place = NONE
            for s in range(1, SLOTS):
                place = jnp.where(offs[s] == o, ranks[s - 1], place)
            own_places[r, o] = place
    for m in OTHERS:
        for r, _ in SENT[m]:
            held[m][r, NONE] = zero

    pl.semaphore_wait(barrier, 8)

    copies = []
    number = 0
    for k, m in enumerate(OTHERS):
        copy = pltpu.make_async_remote_copy(
            src_ref=own_places,
            dst_ref=places[m],
            send_sem=psend_sem.at[k],
            recv_sem=precv_sem.at[k],
            device_id=device(-m),
            device_id_type=pl.DeviceIdType.MESH,
        )
        copy.start()
        copies.append(copy)
    for m in (1, -1, 2, -2, 3, -3, 4):
        for r, count in SENT[m]:
            copy = pltpu.make_async_remote_copy(
                src_ref=own.at[r, pl.ds(0, count)],
                dst_ref=held[m].at[r, pl.ds(0, count)],
                send_sem=send_sem.at[number],
                recv_sem=recv_sem.at[number],
                device_id=device(-m),
                device_id_type=pl.DeviceIdType.MESH,
            )
            copy.start()
            copies.append(copy)
            number += 1
    for copy in copies:
        copy.wait()

    def stored(row, offset):
        m, r = row // 2 - 3, row % 2
        if m == 0:
            return own[r, own_places[r, offset]]
        return held[m][r, places[m][r, offset]]

    def block(a, b):
        if a == b:
            d = stored(a, 0)
            return (d.astype(jnp.float32) + d.T.astype(jnp.float32)).astype(jnp.bfloat16)
        if abs(a - b) > REACH or min(a, b) > LAST:
            return zero
        if a < b:
            return stored(a, b - a)
        return stored(b, a - b).T

    for a in range(ROWS):
        for k in range(LAST + 2):
            lost = k > LAST or k < a
            left[pl.ds(a * BLK, BLK), pl.ds(k * BLK, BLK)] = zero if lost else block(FIRST + a, k)
    for p in range(REACH + 1):
        for k in range(2 * p, LAST + 2):
            for c in range(2):
                j = FIRST + 1 + 2 * p + c
                right[p, pl.ds(k * BLK, BLK), pl.ds(c * BLK, BLK)] = zero if k > LAST else block(k, j)
    for p in range(REACH + 1):
        deep = pl.ds(2 * p * BLK, (LAST + 2 - 2 * p) * BLK)
        got = jnp.dot(left[:, deep], right[p, deep, :], preferred_element_type=jnp.float32).astype(jnp.bfloat16)
        for a in range(ROWS):
            for c in range(2):
                step = 2 * p + c + 1 - a
                if 1 <= step <= STEPS:
                    every[a, step - 1] = got[a * BLK : (a + 1) * BLK, c * BLK : (c + 1) * BLK]
    for a in range(ROWS):
        for t in range(kept.shape[1]):
            step = lax.rem(kept[a, t] - (me * ROWS + a) + block_total, block_total)
            out[a, t] = every[a, jnp.clip(step - 1, 0, STEPS - 1)]


def on_device(upper_vals, upper_cols, result_cols):
    device_total = lax.axis_size("row") * lax.axis_size("col")
    rows, kept_count = result_cols.shape
    places_shape = pltpu.SMEM((ROWS, REACH + 1), jnp.int32)
    copy_total = sum(len(part) for part in SENT.values())

    def kernel(*refs):
        band_kernel(device_total, device_total * ROWS, *refs)

    return pl.pallas_call(
        kernel,
        out_shape=jax.ShapeDtypeStruct((rows, kept_count, BLK, BLK), jnp.bfloat16),
        in_specs=[
            pl.BlockSpec(memory_space=pltpu.VMEM),
            pl.BlockSpec(memory_space=pltpu.SMEM),
            pl.BlockSpec(memory_space=pltpu.SMEM),
        ],
        out_specs=pl.BlockSpec(memory_space=pltpu.VMEM),
        scratch_shapes=[
            *[pltpu.VMEM((ROWS, SLOTS + 1, BLK, BLK), jnp.bfloat16) for _ in OTHERS],
            *[places_shape for _ in OTHERS],
            pltpu.VMEM((ROWS, SLOTS + 1, BLK, BLK), jnp.bfloat16),
            places_shape,
            pltpu.VMEM((ROWS * BLK, (LAST + 2) * BLK), jnp.bfloat16),
            pltpu.VMEM((REACH + 1, (LAST + 2) * BLK, 2 * BLK), jnp.bfloat16),
            pltpu.VMEM((ROWS, STEPS, BLK, BLK), jnp.bfloat16),
            pltpu.SemaphoreType.DMA((copy_total,)),
            pltpu.SemaphoreType.DMA((copy_total,)),
            pltpu.SemaphoreType.DMA((len(OTHERS),)),
            pltpu.SemaphoreType.DMA((len(OTHERS),)),
        ],
        compiler_params=pltpu.CompilerParams(
            collective_id=0, has_side_effects=True, vmem_limit_bytes=40 << 20
        ),
        cost_estimate=pl.CostEstimate(flops=1_200_000_000, bytes_accessed=6_000_000, transcendentals=0),
    )(upper_vals, upper_cols, result_cols)


def solution(mesh):
    in_specs = (
        P(("row", "col"), None, None, None),
        P(("row", "col"), None),
        P(("row", "col"), None),
    )
    out_specs = P(("row", "col"), None, None, None)
    return jax.shard_map(
        on_device, mesh=mesh, in_specs=in_specs, out_specs=out_specs, check_vma=False
    )
```

time: 352 us -> 56.4 us (0.16)
  the two profiles are of different devices: /device:TPU:235 before, /device:TPU:97 now
where the time goes in v1:
time: 56.4 us; the launch traced here: 56.2 us
  Pallas kernels  53.1 us (94%)
  local copies, waits for them, and re-layouts  3.15 us (6%)
    pallas_call x1, Pallas kernels, on_device(): pl.pallas_call(kernel, out_shape=jax.ShapeDtypeStruct((rows, kept_count,...  53.1 us
    unnamed x7, local copies, waits for them, and re-layouts  3.15 us

profile of v1, /device:TPU:97, one launch (start us, length us, event | category | flops | bytes accessed | tf_op | source)
XLA Modules:
  0.0 56.2 jit_solution(18414386942388648613)
XLA Ops:
  0.0 0.0 copy-start
  0.0 1.0 %copy-done = bf16[2,6,128,128]{3,2,1,0:T(8,128)(2,1)S(1)} copy-done((bf16[2,6,128,128]{3,2,1,0:T(8,128)(2,1)S(1)}, bf16[2,6,128,128]{3,2,1,0:T(8,128)(2,1)}, u32[]{:S(2)}) %copy-start) | copy-done | bytes 393240
  1.0 0.0 copy-start.1
  1.0 0.7 %copy-done.1 = s32[2,6]{1,0:T(2,128)S(1)} copy-done((s32[2,6]{1,0:T(2,128)S(1)}, s32[2,6]{1,0:T(2,128)}, u32[]{:S(2)}) %copy-start.1) | copy-done | bytes 72
  1.7 0.0 copy-start.2
  1.7 0.7 %copy-done.2 = s32[2,8]{1,0:T(2,128)S(1)} copy-done((s32[2,8]{1,0:T(2,128)S(1)}, s32[2,8]{1,0:T(2,128)}, u32[]{:S(2)}) %copy-start.2) | copy-done | bytes 88
  2.4 53.1 %shard_map.37 = bf16[2,8,128,128]{3,2,1,0:T(8,128)(2,1)S(1)} custom-call(bf16[2,6,128,128]{3,2,1,0:T(8,128)(2,1)S(1)} %copy-done, s32[2,6]{1,0:T(2,128)S(1)} %copy-done.1, s32[2,8]{1,0:T(2,128)S(1)} %copy-done.2), custom_call_target="tpu_custom_call" | custom-call | flops 1200000000 | bytes 6000000 | tf_op jit(solution)/shard_map/pallas_call | solution.py:146
  55.4 0.8 %copy.5 = bf16[2,8,128,128]{3,2,1,0:T(8,128)(2,1)} copy(bf16[2,8,128,128]{3,2,1,0:T(8,128)(2,1)S(1)} %shard_map.37) | data formatting | bytes 1048576
Async XLA Ops:
  0.0 1.0 %copy-start = (bf16[2,6,128,128]{3,2,1,0:T(8,128)(2,1)S(1)}, bf16[2,6,128,128]{3,2,1,0:T(8,128)(2,1)}, u32[]{:S(2)}) copy-start(bf16[2,6,128,128]{3,2,1,0:T(8,128)(2,1)} %refs_0_.1) | copy-start | bytes 1179652
  1.0 0.7 %copy-start.1 = (s32[2,6]{1,0:T(2,128)S(1)}, s32[2,6]{1,0:T(2,128)}, u32[]{:S(2)}) copy-start(s32[2,6]{1,0:T(2,128)} %refs_1_.1) | copy-start | bytes 148
  1.7 0.7 %copy-start.2 = (s32[2,8]{1,0:T(2,128)S(1)}, s32[2,8]{1,0:T(2,128)}, u32[]{:S(2)}) copy-start(s32[2,8]{1,0:T(2,128)} %refs_2_.1) | copy-start | bytes 196

commit v2 on v1

--- a/solution.py
+++ b/solution.py
@@ -1,3 +1,5 @@
+import functools
+
 import jax
 import jax.numpy as jnp
 from jax import lax
@@ -16,15 +18,47 @@
 BEHIND = (-3, -2, -1)
 AHEAD = (1, 2, 3, 4)
 OTHERS = BEHIND + AHEAD
-SENT = {
-    -3: ((0, 2), (1, 3)),
-    -2: ((0, 4), (1, 5)),
-    -1: ((0, 5), (1, 5)),
-    1: ((0, 6), (1, 6)),
-    2: ((0, 6), (1, 6)),
-    3: ((0, 6), (1, 6)),
-    4: ((0, 6),),
+NEEDED = (
+    {1: 5, 2: 4, 3: 2, -1: 6, -2: 6, -3: 6, -4: 6},
+    {1: 5, 2: 5, 3: 3, -1: 6, -2: 6, -3: 6},
+)
+LANES = 4
+TREES = {
+    (0, 0): {-4: 0, -3: -4, -2: 2, -1: -4, 1: 0, 2: 1, 3: 0},
+    (0, 1): {-3: 1, -2: -1, -1: 3, 1: 0, 2: 3, 3: 0},
+    (1, 0): {-4: 0, -3: -4, -2: 2, -1: 0, 1: 0, 2: -1, 3: -1},
+    (1, 1): {-3: 1, -2: -3, -1: 0, 1: 0, 2: -1, 3: -1},
+    (2, 0): {-4: 0, -3: -4, -2: -1, -1: 0, 1: 0, 2: -2, 3: -1},
+    (2, 1): {-3: 1, -2: 1, -1: 0, 1: 0, 2: 3, 3: -1},
+    (3, 0): {-4: 0, -3: 0, -2: -3, -1: 0, 1: -3, 2: -2, 3: -1},
+    (3, 1): {-3: 0, -2: -1, -1: 0, 1: -3, 2: 3, 3: -1},
 }
+ARRIVALS = {
+    0: ((4, 0), (1, 0), (3, 0), (-3, 0), (1, 1), (3, 1), (-1, 0), (-3, 1), (2, 1), (2, 0), (-1, 1), (-2, 1), (-2, 0)),
+    1: ((-1, 0), (4, 0), (1, 1), (-1, 1), (1, 0), (-3, 1), (2, 0), (2, 1), (3, 1), (-3, 0), (3, 0), (-2, 1), (-2, 0)),
+    2: ((-1, 1), (4, 0), (1, 1), (-1, 0), (1, 0), (3, 1), (-2, 0), (-2, 1), (-3, 1), (-3, 0), (3, 0), (2, 1), (2, 0)),
+    3: ((-3, 1), (-1, 1), (4, 0), (-3, 0), (-1, 0), (1, 1), (-2, 0), (3, 0), (3, 1), (1, 0), (2, 1), (-2, 1), (2, 0)),
+}
+FIRST_SENDS = {
+    0: ((1, 0), (3, 1), (-4, 0), (1, 1), (3, 0)),
+    1: ((-1, 0), (1, 1), (-4, 0), (-1, 1), (1, 0)),
+    2: ((-1, 1), (-1, 0), (-4, 0), (1, 1), (1, 0)),
+    3: ((-3, 0), (-1, 1), (-3, 1), (-1, 0), (-4, 0)),
+}
+
+
+def size(tree, needed, node):
+    below = [size(tree, needed, n) for n, parent in tree.items() if parent == node]
+    return max(below + [needed.get(node, 0)])
+
+
+def hops(lane, distance, r):
+    tree = TREES[(lane + distance) % LANES, r]
+    return [
+        (node + distance, -node, size(tree, NEEDED[r], node))
+        for node, parent in tree.items()
+        if parent == -distance
+    ]
 
 
 def band_kernel(device_total, block_total, vals, cols, kept, out, *scratch):
@@ -61,15 +95,24 @@
                 place = jnp.where(offs[s] == o, ranks[s - 1], place)
             own_places[r, o] = place
     for m in OTHERS:
-        for r, _ in SENT[m]:
+        for r in range(ROWS):
             held[m][r, NONE] = zero
 
     pl.semaphore_wait(barrier, 8)
 
-    copies = []
-    number = 0
+    def remote(source, target, r, count, send, distance, there):
+        return pltpu.make_async_remote_copy(
+            src_ref=source.at[r, pl.ds(0, count)],
+            dst_ref=target.at[r, pl.ds(0, count)],
+            send_sem=send_sem.at[send],
+            recv_sem=recv_sem.at[OTHERS.index(there), r],
+            device_id=device(distance),
+            device_id_type=pl.DeviceIdType.MESH,
+        )
+
+    notes = []
     for k, m in enumerate(OTHERS):
-        copy = pltpu.make_async_remote_copy(
+        note = pltpu.make_async_remote_copy(
             src_ref=own_places,
             dst_ref=places[m],
             send_sem=psend_sem.at[k],
@@ -77,23 +120,34 @@
             device_id=device(-m),
             device_id_type=pl.DeviceIdType.MESH,
         )
-        copy.start()
-        copies.append(copy)
-    for m in (1, -1, 2, -2, 3, -3, 4):
-        for r, count in SENT[m]:
-            copy = pltpu.make_async_remote_copy(
-                src_ref=own.at[r, pl.ds(0, count)],
-                dst_ref=held[m].at[r, pl.ds(0, count)],
-                send_sem=send_sem.at[number],
-                recv_sem=recv_sem.at[number],
-                device_id=device(-m),
-                device_id_type=pl.DeviceIdType.MESH,
-            )
-            copy.start()
-            copies.append(copy)
-            number += 1
-    for copy in copies:
-        copy.wait()
+        note.start()
+        notes.append(note)
+
+    def traffic(lane):
+        sent = []
+
+        def pass_on(m, r, only=None):
+            source = own if m == 0 else held[m]
+            for distance, there, count in hops(lane, m, r):
+                if only in (None, distance):
+                    copy = remote(source, held[there], r, count, len(sent), distance, there)
+                    copy.start()
+                    sent.append(copy)
+
+        for distance, r in FIRST_SENDS[lane]:
+            pass_on(0, r, distance)
+        for m, r in ARRIVALS[lane]:
+            count = size(TREES[(lane + m) % LANES, r], NEEDED[r], -m)
+            remote(own, held[m], r, count, 0, 1, m).wait_recv()
+            pass_on(m, r)
+        for copy in sent:
+            copy.wait_send()
+
+    lane_here = lax.rem(me, LANES)
+    for lane in range(LANES):
+        pl.when(lane_here == lane)(functools.partial(traffic, lane))
+    for note in notes:
+        note.wait()
 
     def stored(row, offset):
         m, r = row // 2 - 3, row % 2
@@ -138,7 +192,9 @@
     device_total = lax.axis_size("row") * lax.axis_size("col")
     rows, kept_count = result_cols.shape
     places_shape = pltpu.SMEM((ROWS, REACH + 1), jnp.int32)
-    copy_total = sum(len(part) for part in SENT.values())
+    most_sent = max(
+        sum(len(hops(lane, m, r)) for m, r in ARRIVALS[lane] + ((0, 0), (0, 1))) for lane in range(LANES)
+    )
 
     def kernel(*refs):
         band_kernel(device_total, device_total * ROWS, *refs)
@@ -160,8 +216,8 @@
             pltpu.VMEM((ROWS * BLK, (LAST + 2) * BLK), jnp.bfloat16),
             pltpu.VMEM((REACH + 1, (LAST + 2) * BLK, 2 * BLK), jnp.bfloat16),
             pltpu.VMEM((ROWS, STEPS, BLK, BLK), jnp.bfloat16),
-            pltpu.SemaphoreType.DMA((copy_total,)),
-            pltpu.SemaphoreType.DMA((copy_total,)),
+            pltpu.SemaphoreType.DMA((most_sent,)),
+            pltpu.SemaphoreType.DMA((len(OTHERS), ROWS)),
             pltpu.SemaphoreType.DMA((len(OTHERS),)),
             pltpu.SemaphoreType.DMA((len(OTHERS),)),
         ],

time: 56.4 us -> 37.8 us (0.67)
  the two profiles are of different devices: /device:TPU:97 before, /device:TPU:8 now
where the time goes in v2:
time: 37.8 us; the launch traced here: 37.3 us
  Pallas kernels  34.1 us (90%)
  local copies, waits for them, and re-layouts  3.15 us (8%)
    pallas_call x1, Pallas kernels, on_device(): pl.pallas_call(kernel, out_shape=jax.ShapeDtypeStruct((rows, kept_count,...  34.1 us
    unnamed x7, local copies, waits for them, and re-layouts  3.15 us

profile of v2, /device:TPU:8, one launch (start us, length us, event | category | flops | bytes accessed | tf_op | source)
XLA Modules:
  0.0 37.3 jit_solution(1114027473501225374)
XLA Ops:
  0.0 0.0 copy-start
  0.0 1.0 %copy-done = bf16[2,6,128,128]{3,2,1,0:T(8,128)(2,1)S(1)} copy-done((bf16[2,6,128,128]{3,2,1,0:T(8,128)(2,1)S(1)}, bf16[2,6,128,128]{3,2,1,0:T(8,128)(2,1)}, u32[]{:S(2)}) %copy-start) | copy-done | bytes 393240
  1.0 0.0 copy-start.1
  1.0 0.7 %copy-done.1 = s32[2,6]{1,0:T(2,128)S(1)} copy-done((s32[2,6]{1,0:T(2,128)S(1)}, s32[2,6]{1,0:T(2,128)}, u32[]{:S(2)}) %copy-start.1) | copy-done | bytes 72
  1.7 0.0 copy-start.2
  1.7 0.7 %copy-done.2 = s32[2,8]{1,0:T(2,128)S(1)} copy-done((s32[2,8]{1,0:T(2,128)S(1)}, s32[2,8]{1,0:T(2,128)}, u32[]{:S(2)}) %copy-start.2) | copy-done | bytes 88
  2.4 34.1 %shard_map.37 = bf16[2,8,128,128]{3,2,1,0:T(8,128)(2,1)S(1)} custom-call(bf16[2,6,128,128]{3,2,1,0:T(8,128)(2,1)S(1)} %copy-done, s32[2,6]{1,0:T(2,128)S(1)} %copy-done.1, s32[2,8]{1,0:T(2,128)S(1)} %copy-done.2), custom_call_target="tpu_custom_call" | custom-call | flops 1200000000 | bytes 6000000 | tf_op jit(solution)/shard_map/pallas_call | solution.py:202
  36.5 0.8 %copy.5 = bf16[2,8,128,128]{3,2,1,0:T(8,128)(2,1)} copy(bf16[2,8,128,128]{3,2,1,0:T(8,128)(2,1)S(1)} %shard_map.37) | data formatting | bytes 1048576
Async XLA Ops:
  0.0 1.0 %copy-start = (bf16[2,6,128,128]{3,2,1,0:T(8,128)(2,1)S(1)}, bf16[2,6,128,128]{3,2,1,0:T(8,128)(2,1)}, u32[]{:S(2)}) copy-start(bf16[2,6,128,128]{3,2,1,0:T(8,128)(2,1)} %refs_0_.1) | copy-start | bytes 1179652
  1.0 0.7 %copy-start.1 = (s32[2,6]{1,0:T(2,128)S(1)}, s32[2,6]{1,0:T(2,128)}, u32[]{:S(2)}) copy-start(s32[2,6]{1,0:T(2,128)} %refs_1_.1) | copy-start | bytes 148
  1.7 0.7 %copy-start.2 = (s32[2,8]{1,0:T(2,128)S(1)}, s32[2,8]{1,0:T(2,128)}, u32[]{:S(2)}) copy-start(s32[2,8]{1,0:T(2,128)} %refs_2_.1) | copy-start | bytes 196

commit v3 on v2

--- a/solution.py
+++ b/solution.py
@@ -61,10 +61,11 @@
     ]
 
 
-def band_kernel(device_total, block_total, vals, cols, kept, out, *scratch):
+def band_kernel(device_total, block_total, vals_hbm, cols_hbm, kept_hbm, out, *scratch):
     held = dict(zip(OTHERS, scratch[:7]))
     places = dict(zip(OTHERS, scratch[7:14]))
-    own, own_places, left, right, every, send_sem, recv_sem, psend_sem, precv_sem = scratch[14:]
+    own, own_places, left, right, every, vals, cols, kept = scratch[14:22]
+    send_sem, recv_sem, psend_sem, precv_sem, fetch_sem = scratch[22:]
     inner = lax.axis_size("col")
     me = lax.axis_index("row") * inner + lax.axis_index("col")
 
@@ -76,7 +77,19 @@
     for m in (-4, -3, -2, -1, 1, 2, 3, 4):
         pl.semaphore_signal(barrier, inc=1, device_id=device(m), device_id_type=pl.DeviceIdType.MESH)
 
+    fetches = [
+        pltpu.make_async_copy(source, target, fetch_sem.at[k])
+        for k, (source, target) in enumerate(((cols_hbm, cols), (vals_hbm, vals), (kept_hbm, kept)))
+    ]
+    for fetch in fetches:
+        fetch.start()
+
     zero = jnp.zeros((BLK, BLK), jnp.bfloat16)
+    for m in OTHERS:
+        for r in range(ROWS):
+            held[m][r, NONE] = zero
+    fetches[0].wait()
+    fetches[1].wait()
     for r in range(ROWS):
         offs = [lax.rem(cols[r, s] - (me * ROWS + r) + block_total, block_total) for s in range(SLOTS)]
         ranks = [
@@ -94,9 +107,6 @@
             for s in range(1, SLOTS):
                 place = jnp.where(offs[s] == o, ranks[s - 1], place)
             own_places[r, o] = place
-    for m in OTHERS:
-        for r in range(ROWS):
-            held[m][r, NONE] = zero
 
     pl.semaphore_wait(barrier, 8)
 
@@ -110,19 +120,6 @@
             device_id_type=pl.DeviceIdType.MESH,
         )
 
-    notes = []
-    for k, m in enumerate(OTHERS):
-        note = pltpu.make_async_remote_copy(
-            src_ref=own_places,
-            dst_ref=places[m],
-            send_sem=psend_sem.at[k],
-            recv_sem=precv_sem.at[k],
-            device_id=device(-m),
-            device_id_type=pl.DeviceIdType.MESH,
-        )
-        note.start()
-        notes.append(note)
-
     def traffic(lane):
         sent = []
 
@@ -136,18 +133,31 @@
 
         for distance, r in FIRST_SENDS[lane]:
             pass_on(0, r, distance)
+        notes = []
+        for k, m in enumerate(OTHERS):
+            note = pltpu.make_async_remote_copy(
+                src_ref=own_places,
+                dst_ref=places[m],
+                send_sem=psend_sem.at[k],
+                recv_sem=precv_sem.at[k],
+                device_id=device(-m),
+                device_id_type=pl.DeviceIdType.MESH,
+            )
+            note.start()
+            notes.append(note)
         for m, r in ARRIVALS[lane]:
             count = size(TREES[(lane + m) % LANES, r], NEEDED[r], -m)
             remote(own, held[m], r, count, 0, 1, m).wait_recv()
             pass_on(m, r)
         for copy in sent:
             copy.wait_send()
+        for note in notes:
+            note.wait()
 
     lane_here = lax.rem(me, LANES)
     for lane in range(LANES):
         pl.when(lane_here == lane)(functools.partial(traffic, lane))
-    for note in notes:
-        note.wait()
+    fetches[2].wait()
 
     def stored(row, offset):
         m, r = row // 2 - 3, row % 2
@@ -203,9 +213,9 @@
         kernel,
         out_shape=jax.ShapeDtypeStruct((rows, kept_count, BLK, BLK), jnp.bfloat16),
         in_specs=[
-            pl.BlockSpec(memory_space=pltpu.VMEM),
-            pl.BlockSpec(memory_space=pltpu.SMEM),
-            pl.BlockSpec(memory_space=pltpu.SMEM),
+            pl.BlockSpec(memory_space=pltpu.HBM),
+            pl.BlockSpec(memory_space=pltpu.HBM),
+            pl.BlockSpec(memory_space=pltpu.HBM),
         ],
         out_specs=pl.BlockSpec(memory_space=pltpu.VMEM),
         scratch_shapes=[
@@ -216,16 +226,20 @@
             pltpu.VMEM((ROWS * BLK, (LAST + 2) * BLK), jnp.bfloat16),
             pltpu.VMEM((REACH + 1, (LAST + 2) * BLK, 2 * BLK), jnp.bfloat16),
             pltpu.VMEM((ROWS, STEPS, BLK, BLK), jnp.bfloat16),
+            pltpu.VMEM(upper_vals.shape, upper_vals.dtype),
+            pltpu.SMEM(upper_cols.shape, upper_cols.dtype),
+            pltpu.SMEM(result_cols.shape, result_cols.dtype),
             pltpu.SemaphoreType.DMA((most_sent,)),
             pltpu.SemaphoreType.DMA((len(OTHERS), ROWS)),
             pltpu.SemaphoreType.DMA((len(OTHERS),)),
             pltpu.SemaphoreType.DMA((len(OTHERS),)),
+            pltpu.SemaphoreType.DMA((3,)),
         ],
         compiler_params=pltpu.CompilerParams(
             collective_id=0, has_side_effects=True, vmem_limit_bytes=40 << 20
         ),
         cost_estimate=pl.CostEstimate(flops=1_200_000_000, bytes_accessed=6_000_000, transcendentals=0),
-    )(upper_vals, upper_cols, result_cols)
+    )(*(pltpu.with_memory_space_constraint(x, pltpu.HBM) for x in (upper_vals, upper_cols, result_cols)))
 
 
 def solution(mesh):

time: 37.8 us -> 34.7 us (0.918)
  local copies, waits for them, and re-layouts: 3.15 us -> 0.8 us
  Pallas kernels: 34.1 us -> 33.4 us
    unnamed x7 -> x1, local copies, waits for them, and re-layouts: 3.15 us -> 0.8 us
    pallas_call x1, Pallas kernels: 34.1 us -> 33.4 us  [on_device(): pl.pallas_call(kernel, out_shape=jax.ShapeDtypeStruct((rows, kept_count,...]
where the time goes in v3:
time: 34.7 us; the launch traced here: 34.3 us
  Pallas kernels  33.4 us (96%)
  local copies, waits for them, and re-layouts  0.8 us (2%)
    pallas_call x1, Pallas kernels, on_device(): pl.pallas_call(kernel, out_shape=jax.ShapeDtypeStruct((rows, kept_count,...  33.4 us
    unnamed x1, local copies, waits for them, and re-layouts  0.8 us

profile of v3, /device:TPU:8, one launch (start us, length us, event | category | flops | bytes accessed | tf_op | source)
XLA Modules:
  0.0 34.3 jit_solution(14179881270010702003)
XLA Ops:
  0.0 33.4 %shard_map.37 = bf16[2,8,128,128]{3,2,1,0:T(8,128)(2,1)S(1)} custom-call(bf16[2,6,128,128]{3,2,1,0:T(8,128)(2,1)} %refs_0_.1, s32[2,6]{1,0:T(2,128)} %refs_1_.1, s32[2,8]{1,0:T(2,128)} %refs_2_.1), custom_call_target="tpu_custom_call" | custom-call | flops 1200000000 | bytes 6000000 | tf_op jit(solution)/shard_map/pallas_call | solution.py:212
  33.5 0.8 %copy.5 = bf16[2,8,128,128]{3,2,1,0:T(8,128)(2,1)} copy(bf16[2,8,128,128]{3,2,1,0:T(8,128)(2,1)S(1)} %shard_map.37) | data formatting | bytes 1048576

commit v4 on v3

--- a/solution.py
+++ b/solution.py
@@ -15,6 +15,7 @@
 STEPS = 2 * REACH
 FIRST = REACH - 1
 LAST = 2 * REACH
+PAIRS = REACH + 1
 BEHIND = (-3, -2, -1)
 AHEAD = (1, 2, 3, 4)
 OTHERS = BEHIND + AHEAD
@@ -62,10 +63,10 @@
 
 
 def band_kernel(device_total, block_total, vals_hbm, cols_hbm, kept_hbm, out, *scratch):
-    held = dict(zip(OTHERS, scratch[:7]))
-    places = dict(zip(OTHERS, scratch[7:14]))
-    own, own_places, left, right, every, vals, cols, kept = scratch[14:22]
-    send_sem, recv_sem, psend_sem, precv_sem, fetch_sem = scratch[22:]
+    held = {(m, r): scratch[i * ROWS + r] for i, m in enumerate((0, *OTHERS)) for r in range(ROWS)}
+    places = dict(zip((0, *OTHERS), scratch[16:24]))
+    left, right, sums, every, vals, cols, kept = scratch[24:31]
+    send_sem, recv_sem, psend_sem, precv_sem, fetch_sem = scratch[31:]
     inner = lax.axis_size("col")
     me = lax.axis_index("row") * inner + lax.axis_index("col")
 
@@ -76,7 +77,6 @@
     barrier = pltpu.get_barrier_semaphore()
     for m in (-4, -3, -2, -1, 1, 2, 3, 4):
         pl.semaphore_signal(barrier, inc=1, device_id=device(m), device_id_type=pl.DeviceIdType.MESH)
-
     fetches = [
         pltpu.make_async_copy(source, target, fetch_sem.at[k])
         for k, (source, target) in enumerate(((cols_hbm, cols), (vals_hbm, vals), (kept_hbm, kept)))
@@ -85,58 +85,142 @@
         fetch.start()
 
     zero = jnp.zeros((BLK, BLK), jnp.bfloat16)
-    for m in OTHERS:
+    for m in (0, *OTHERS):
         for r in range(ROWS):
-            held[m][r, NONE] = zero
+            held[m, r][NONE] = zero
     fetches[0].wait()
-    fetches[1].wait()
+    slots = []
     for r in range(ROWS):
         offs = [lax.rem(cols[r, s] - (me * ROWS + r) + block_total, block_total) for s in range(SLOTS)]
         ranks = [
             sum((offs[t] > offs[s]).astype(jnp.int32) for t in range(1, SLOTS) if t != s)
             for s in range(1, SLOTS)
         ]
-        for j in range(SLOTS - 1):
-            slot = sum(s * (ranks[s - 1] == j).astype(jnp.int32) for s in range(1, SLOTS))
-            own[r, j] = vals[r, jnp.minimum(slot, SLOTS - 1)]
-        own[r, SLOTS - 1] = vals[r, 0]
-        own[r, NONE] = zero
-        own_places[r, 0] = SLOTS - 1
+        slots.append(
+            [
+                jnp.minimum(
+                    sum(s * (ranks[s - 1] == j).astype(jnp.int32) for s in range(1, SLOTS)), SLOTS - 1
+                )
+                for j in range(SLOTS - 1)
+            ]
+        )
+        places[0][r, 0] = SLOTS - 1
         for o in range(1, REACH + 1):
             place = NONE
             for s in range(1, SLOTS):
                 place = jnp.where(offs[s] == o, ranks[s - 1], place)
-            own_places[r, o] = place
+            places[0][r, o] = place
+    fetches[1].wait()
+    for r in range(ROWS):
+        for j in range(SLOTS - 1):
+            held[0, r][j] = vals[r, slots[r][j]]
+        held[0, r][SLOTS - 1] = vals[r, 0]
+    fetches[2].wait()
 
     pl.semaphore_wait(barrier, 8)
 
     def remote(source, target, r, count, send, distance, there):
         return pltpu.make_async_remote_copy(
-            src_ref=source.at[r, pl.ds(0, count)],
-            dst_ref=target.at[r, pl.ds(0, count)],
+            src_ref=source.at[pl.ds(0, count)],
+            dst_ref=target.at[pl.ds(0, count)],
             send_sem=send_sem.at[send],
             recv_sem=recv_sem.at[OTHERS.index(there), r],
             device_id=device(distance),
             device_id_type=pl.DeviceIdType.MESH,
         )
 
+    def stored(row, offset):
+        m, r = row // 2 - 3, row % 2
+        return held[m, r][places[m][r, offset]]
+
+    def block(a, b):
+        if a == b:
+            d = stored(a, 0)
+            return (d.astype(jnp.float32) + d.T.astype(jnp.float32)).astype(jnp.bfloat16)
+        if a < b:
+            return stored(a, b - a)
+        return stored(b, a - b).T
+
+    def source(a, b):
+        row = min(a, b)
+        if abs(a - b) > REACH or row > LAST:
+            return None
+        return (row // 2 - 3, row % 2)
+
     def traffic(lane):
         sent = []
+        here = {(0, 0), (0, 1), None}
+        made = set()
+        summed = {p: set() for p in range(PAIRS)}
+        order = ARRIVALS[lane]
+        last_relay = max(i for i, (m, r) in enumerate(order) if hops(lane, m, r))
 
         def pass_on(m, r, only=None):
-            source = own if m == 0 else held[m]
             for distance, there, count in hops(lane, m, r):
                 if only in (None, distance):
-                    copy = remote(source, held[there], r, count, len(sent), distance, there)
+                    copy = remote(held[m, r], held[there, r], r, count, len(sent), distance, there)
                     copy.start()
                     sent.append(copy)
+
+        def arrive(m, r):
+            count = size(TREES[(lane + m) % LANES, r], NEEDED[r], -m)
+            remote(held[0, r], held[m, r], r, count, 0, 1, m).wait_recv()
+            here.add((m, r))
+
+        def place(key, ref, at, a, b):
+            if key not in made and source(a, b) in here:
+                ref[at] = zero if source(a, b) is None else block(a, b)
+                made.add(key)
+
+        def assemble():
+            for k in range(LAST + 2):
+                for a in range(ROWS):
+                    at = (pl.ds(a * BLK, BLK), pl.ds(k * BLK, BLK))
+                    place(("left", a, k), left, at, FIRST + a, k)
+                for p in range(k // 2 + 1):
+                    for c in range(2):
+                        at = (p, pl.ds(k * BLK, BLK), pl.ds(c * BLK, BLK))
+                        place(("right", p, k, c), right, at, k, FIRST + 1 + 2 * p + c)
+
+        def multiply():
+            for p in range(PAIRS):
+                ready = [
+                    q
+                    for q in range(p, PAIRS)
+                    if q not in summed[p]
+                    and all(("left", a, k) in made for a in range(ROWS) for k in (2 * q, 2 * q + 1))
+                    and all(("right", p, k, c) in made for k in (2 * q, 2 * q + 1) for c in range(2))
+                ]
+                if not ready:
+                    continue
+                runs = []
+                for q in ready:
+                    if runs and runs[-1][1] == q:
+                        runs[-1][1] = q + 1
+                    else:
+                        runs.append([q, q + 1])
+                total = sums[p] if summed[p] else None
+                for low, high in runs:
+                    deep = pl.ds(2 * low * BLK, 2 * (high - low) * BLK)
+                    part = jnp.dot(left[:, deep], right[p, deep, :], preferred_element_type=jnp.float32)
+                    total = part if total is None else total + part
+                summed[p].update(ready)
+                if len(summed[p]) < PAIRS - p:
+                    sums[p] = total
+                    continue
+                got = total.astype(jnp.bfloat16)
+                for a in range(ROWS):
+                    for c in range(2):
+                        step = 2 * p + c + 1 - a
+                        if 1 <= step <= STEPS:
+                            every[a, step - 1] = got[a * BLK : (a + 1) * BLK, c * BLK : (c + 1) * BLK]
 
         for distance, r in FIRST_SENDS[lane]:
             pass_on(0, r, distance)
         notes = []
         for k, m in enumerate(OTHERS):
             note = pltpu.make_async_remote_copy(
-                src_ref=own_places,
+                src_ref=places[0],
                 dst_ref=places[m],
                 send_sem=psend_sem.at[k],
                 recv_sem=precv_sem.at[k],
@@ -145,53 +229,24 @@
             )
             note.start()
             notes.append(note)
-        for m, r in ARRIVALS[lane]:
-            count = size(TREES[(lane + m) % LANES, r], NEEDED[r], -m)
-            remote(own, held[m], r, count, 0, 1, m).wait_recv()
+        assemble()
+        for m, r in order[: last_relay + 1]:
+            arrive(m, r)
             pass_on(m, r)
+        for note in notes:
+            note.wait()
+        for m, r in order[last_relay + 1 :]:
+            assemble()
+            multiply()
+            arrive(m, r)
+        assemble()
+        multiply()
         for copy in sent:
             copy.wait_send()
-        for note in notes:
-            note.wait()
 
     lane_here = lax.rem(me, LANES)
     for lane in range(LANES):
         pl.when(lane_here == lane)(functools.partial(traffic, lane))
-    fetches[2].wait()
-
-    def stored(row, offset):
-        m, r = row // 2 - 3, row % 2
-        if m == 0:
-            return own[r, own_places[r, offset]]
-        return held[m][r, places[m][r, offset]]
-
-    def block(a, b):
-        if a == b:
-            d = stored(a, 0)
-            return (d.astype(jnp.float32) + d.T.astype(jnp.float32)).astype(jnp.bfloat16)
-        if abs(a - b) > REACH or min(a, b) > LAST:
-            return zero
-        if a < b:
-            return stored(a, b - a)
-        return stored(b, a - b).T
-
-    for a in range(ROWS):
-        for k in range(LAST + 2):
-            lost = k > LAST or k < a
-            left[pl.ds(a * BLK, BLK), pl.ds(k * BLK, BLK)] = zero if lost else block(FIRST + a, k)
-    for p in range(REACH + 1):
-        for k in range(2 * p, LAST + 2):
-            for c in range(2):
-                j = FIRST + 1 + 2 * p + c
-                right[p, pl.ds(k * BLK, BLK), pl.ds(c * BLK, BLK)] = zero if k > LAST else block(k, j)
-    for p in range(REACH + 1):
-        deep = pl.ds(2 * p * BLK, (LAST + 2 - 2 * p) * BLK)
-        got = jnp.dot(left[:, deep], right[p, deep, :], preferred_element_type=jnp.float32).astype(jnp.bfloat16)
-        for a in range(ROWS):
-            for c in range(2):
-                step = 2 * p + c + 1 - a
-                if 1 <= step <= STEPS:
-                    every[a, step - 1] = got[a * BLK : (a + 1) * BLK, c * BLK : (c + 1) * BLK]
     for a in range(ROWS):
         for t in range(kept.shape[1]):
             step = lax.rem(kept[a, t] - (me * ROWS + a) + block_total, block_total)
@@ -219,12 +274,11 @@
         ],
         out_specs=pl.BlockSpec(memory_space=pltpu.VMEM),
         scratch_shapes=[
-            *[pltpu.VMEM((ROWS, SLOTS + 1, BLK, BLK), jnp.bfloat16) for _ in OTHERS],
-            *[places_shape for _ in OTHERS],
-            pltpu.VMEM((ROWS, SLOTS + 1, BLK, BLK), jnp.bfloat16),
-            places_shape,
-            pltpu.VMEM((ROWS * BLK, (LAST + 2) * BLK), jnp.bfloat16),
-            pltpu.VMEM((REACH + 1, (LAST + 2) * BLK, 2 * BLK), jnp.bfloat16),
+            *[pltpu.VMEM((SLOTS + 1, BLK, BLK), jnp.bfloat16) for _ in range(ROWS * (1 + len(OTHERS)))],
+            *[places_shape for _ in range(1 + len(OTHERS))],
+            pltpu.VMEM((ROWS * BLK, 2 * PAIRS * BLK), jnp.bfloat16),
+            pltpu.VMEM((PAIRS, 2 * PAIRS * BLK, 2 * BLK), jnp.bfloat16),
+            pltpu.VMEM((PAIRS, ROWS * BLK, 2 * BLK), jnp.float32),
             pltpu.VMEM((ROWS, STEPS, BLK, BLK), jnp.bfloat16),
             pltpu.VMEM(upper_vals.shape, upper_vals.dtype),
             pltpu.SMEM(upper_cols.shape, upper_cols.dtype),

time: 34.7 us -> 33.1 us (0.954)
  Pallas kernels: 33.4 us -> 31.9 us
    pallas_call x1, Pallas kernels: 33.4 us -> 31.9 us  [on_device(): pl.pallas_call(kernel, out_shape=jax.ShapeDtypeStruct((rows, kept_count,...]
where the time goes in v4:
time: 33.1 us; the launch traced here: 32.7 us
  Pallas kernels  31.9 us (96%)
  local copies, waits for them, and re-layouts  0.8 us (2%)
    pallas_call x1, Pallas kernels, on_device(): pl.pallas_call(kernel, out_shape=jax.ShapeDtypeStruct((rows, kept_count,...  31.9 us
    unnamed x1, local copies, waits for them, and re-layouts  0.8 us

profile of v4, /device:TPU:8, one launch (start us, length us, event | category | flops | bytes accessed | tf_op | source)
XLA Modules:
  0.0 32.7 jit_solution(8313624909375212981)
XLA Ops:
  0.0 31.9 %shard_map.37 = bf16[2,8,128,128]{3,2,1,0:T(8,128)(2,1)S(1)} custom-call(bf16[2,6,128,128]{3,2,1,0:T(8,128)(2,1)} %refs_0_.1, s32[2,6]{1,0:T(2,128)} %refs_1_.1, s32[2,8]{1,0:T(2,128)} %refs_2_.1), custom_call_target="tpu_custom_call" | custom-call | flops 1200000000 | bytes 6000000 | tf_op jit(solution)/shard_map/pallas_call | solution.py:267
  31.9 0.8 %copy.5 = bf16[2,8,128,128]{3,2,1,0:T(8,128)(2,1)} copy(bf16[2,8,128,128]{3,2,1,0:T(8,128)(2,1)S(1)} %shard_map.37) | data formatting | bytes 1048576

commit v5 on v4

--- a/solution.py
+++ b/solution.py
@@ -23,29 +23,30 @@
     {1: 5, 2: 4, 3: 2, -1: 6, -2: 6, -3: 6, -4: 6},
     {1: 5, 2: 5, 3: 3, -1: 6, -2: 6, -3: 6},
 )
-LANES = 4
 TREES = {
-    (0, 0): {-4: 0, -3: -4, -2: 2, -1: -4, 1: 0, 2: 1, 3: 0},
-    (0, 1): {-3: 1, -2: -1, -1: 3, 1: 0, 2: 3, 3: 0},
-    (1, 0): {-4: 0, -3: -4, -2: 2, -1: 0, 1: 0, 2: -1, 3: -1},
-    (1, 1): {-3: 1, -2: -3, -1: 0, 1: 0, 2: -1, 3: -1},
-    (2, 0): {-4: 0, -3: -4, -2: -1, -1: 0, 1: 0, 2: -2, 3: -1},
-    (2, 1): {-3: 1, -2: 1, -1: 0, 1: 0, 2: 3, 3: -1},
-    (3, 0): {-4: 0, -3: 0, -2: -3, -1: 0, 1: -3, 2: -2, 3: -1},
-    (3, 1): {-3: 0, -2: -1, -1: 0, 1: -3, 2: 3, 3: -1},
+    (0, 0): {3: 0, -3: -4, 2: 1, -2: -1, 1: 0, -1: -4, -4: 0},
+    (0, 1): {3: 0, 2: 3, -3: 1, 1: 0, -1: 3, -2: -3},
+    (1, 0): {-4: 0, 2: -1, 1: 0, -2: -3, 3: -1, -3: -4, -1: 0},
+    (1, 1): {-2: 2, 3: -1, 2: 1, -3: 1, 1: 0, -1: 0},
+    (2, 0): {2: -2, -3: -4, 3: -1, -4: 0, 1: -2, -2: -1, -1: 0},
+    (2, 1): {1: 0, 3: -1, -3: 1, -2: 1, 2: 3, -1: 0},
+    (3, 0): {3: -1, 1: -3, -4: 0, 2: -2, -3: 0, -1: 0, -2: -1},
+    (3, 1): {3: -1, -2: -3, 1: -3, -3: 0, 2: 3, -1: 0},
 }
 ARRIVALS = {
-    0: ((4, 0), (1, 0), (3, 0), (-3, 0), (1, 1), (3, 1), (-1, 0), (-3, 1), (2, 1), (2, 0), (-1, 1), (-2, 1), (-2, 0)),
-    1: ((-1, 0), (4, 0), (1, 1), (-1, 1), (1, 0), (-3, 1), (2, 0), (2, 1), (3, 1), (-3, 0), (3, 0), (-2, 1), (-2, 0)),
-    2: ((-1, 1), (4, 0), (1, 1), (-1, 0), (1, 0), (3, 1), (-2, 0), (-2, 1), (-3, 1), (-3, 0), (3, 0), (2, 1), (2, 0)),
-    3: ((-3, 1), (-1, 1), (4, 0), (-3, 0), (-1, 0), (1, 1), (-2, 0), (3, 0), (3, 1), (1, 0), (2, 1), (-2, 1), (2, 0)),
+    0: ((1, 1, 0), (4, 0, 0), (3, 1, 0), (1, 0, 0), (3, 0, 0), (4, 0, 1), (1, 1, 1), (3, 1, 1), (-3, 1, 0), (1, 0, 1), (3, 0, 1), (-1, 1, 0), (2, 0, 0), (-3, 0, 0), (2, 1, 0), (-1, 0, 0), (2, 0, 1), (2, 1, 1), (-1, 1, 1), (-2, 1, 0), (-1, 0, 1), (-2, 1, 1), (-2, 0, 0), (-2, 0, 1)),
+    1: ((-1, 0, 0), (1, 0, 0), (4, 0, 0), (-1, 1, 0), (1, 1, 0), (4, 0, 1), (-1, 0, 1), (-3, 0, 0), (1, 0, 1), (-1, 1, 1), (1, 1, 1), (3, 1, 0), (-3, 1, 0), (2, 1, 0), (2, 0, 0), (3, 0, 0), (2, 0, 1), (-3, 1, 1), (3, 1, 1), (3, 0, 1), (-2, 1, 0), (-2, 0, 0), (2, 1, 1), (-2, 0, 1), (-2, 1, 1)),
+    2: ((-1, 0, 0), (1, 0, 0), (4, 0, 0), (-1, 1, 0), (1, 1, 0), (4, 0, 1), (-1, 0, 1), (-3, 0, 0), (1, 0, 1), (-1, 1, 1), (1, 1, 1), (3, 1, 0), (-3, 1, 0), (-2, 0, 0), (-2, 1, 0), (3, 0, 0), (-2, 1, 1), (3, 1, 1), (-3, 1, 1), (3, 0, 1), (2, 0, 0), (-2, 0, 1), (2, 0, 1), (2, 1, 0), (2, 1, 1)),
+    3: ((-3, 1, 0), (-1, 1, 0), (4, 0, 0), (-3, 0, 0), (-1, 1, 1), (4, 0, 1), (-3, 1, 1), (3, 0, 0), (1, 1, 0), (1, 0, 0), (3, 1, 0), (-2, 1, 0), (3, 0, 1), (-2, 0, 0), (3, 1, 1), (1, 0, 1), (-2, 0, 1), (-2, 1, 1), (1, 1, 1), (-1, 0, 0), (2, 0, 0), (2, 1, 0), (-1, 0, 1), (2, 1, 1), (2, 0, 1)),
 }
 FIRST_SENDS = {
-    0: ((1, 0), (3, 1), (-4, 0), (1, 1), (3, 0)),
-    1: ((-1, 0), (1, 1), (-4, 0), (-1, 1), (1, 0)),
-    2: ((-1, 1), (-1, 0), (-4, 0), (1, 1), (1, 0)),
-    3: ((-3, 0), (-1, 1), (-3, 1), (-1, 0), (-4, 0)),
+    0: ((3, 1, 0), (3, 0, 0), (3, 1, 1), (1, 0, 0), (1, 1, 0), (1, 0, 1), (1, 1, 1), (-4, 0, 0), (-4, 0, 1)),
+    1: ((-4, 0, 0), (-4, 0, 1), (1, 0, 0), (1, 1, 0), (1, 0, 1), (1, 1, 1), (-1, 1, 0), (-1, 0, 0), (-1, 1, 1), (-1, 0, 1)),
+    2: ((-4, 0, 0), (-4, 0, 1), (1, 1, 0), (1, 1, 1), (-1, 0, 0), (-1, 1, 0), (-1, 0, 1), (-1, 1, 1)),
+    3: ((-4, 0, 0), (-4, 0, 1), (-3, 1, 0), (-3, 0, 0), (-3, 1, 1), (-3, 0, 1), (-1, 0, 0), (-1, 1, 0), (-1, 0, 1), (-1, 1, 1)),
 }
+LANES = 4
+FRONT = 3
 
 
 def size(tree, needed, node):
@@ -53,13 +54,18 @@
     return max(below + [needed.get(node, 0)])
 
 
-def hops(lane, distance, r):
+def parts(count):
+    return [(0, count)] if count <= FRONT else [(0, FRONT), (FRONT, count - FRONT)]
+
+
+def hops(lane, distance, r, part):
     tree = TREES[(lane + distance) % LANES, r]
-    return [
-        (node + distance, -node, size(tree, NEEDED[r], node))
-        for node, parent in tree.items()
-        if parent == -distance
-    ]
+    found = []
+    for node, parent in tree.items():
+        spans = parts(size(tree, NEEDED[r], node))
+        if parent == -distance and part < len(spans):
+            found.append((node + distance, -node, spans[part]))
+    return found
 
 
 def band_kernel(device_total, block_total, vals_hbm, cols_hbm, kept_hbm, out, *scratch):
@@ -119,12 +125,12 @@
 
     pl.semaphore_wait(barrier, 8)
 
-    def remote(source, target, r, count, send, distance, there):
+    def remote(source, target, r, span, send, distance, there):
         return pltpu.make_async_remote_copy(
-            src_ref=source.at[pl.ds(0, count)],
-            dst_ref=target.at[pl.ds(0, count)],
+            src_ref=source.at[pl.ds(*span)],
+            dst_ref=target.at[pl.ds(*span)],
             send_sem=send_sem.at[send],
-            recv_sem=recv_sem.at[OTHERS.index(there), r],
+            recv_sem=recv_sem.at[OTHERS.index(there), r, 0 if span[0] == 0 else 1],
             device_id=device(distance),
             device_id_type=pl.DeviceIdType.MESH,
         )
@@ -153,19 +159,22 @@
         made = set()
         summed = {p: set() for p in range(PAIRS)}
         order = ARRIVALS[lane]
-        last_relay = max(i for i, (m, r) in enumerate(order) if hops(lane, m, r))
-
-        def pass_on(m, r, only=None):
-            for distance, there, count in hops(lane, m, r):
+        last_relay = max(i for i, item in enumerate(order) if hops(lane, *item))
+        missing = {item: sum(item == (m, r) for m, r, _ in order) for item in {(m, r) for m, r, _ in order}}
+
+        def pass_on(m, r, part, only=None):
+            for distance, there, span in hops(lane, m, r, part):
                 if only in (None, distance):
-                    copy = remote(held[m, r], held[there, r], r, count, len(sent), distance, there)
+                    copy = remote(held[m, r], held[there, r], r, span, len(sent), distance, there)
                     copy.start()
                     sent.append(copy)
 
-        def arrive(m, r):
-            count = size(TREES[(lane + m) % LANES, r], NEEDED[r], -m)
-            remote(held[0, r], held[m, r], r, count, 0, 1, m).wait_recv()
-            here.add((m, r))
+        def arrive(m, r, part):
+            span = parts(size(TREES[(lane + m) % LANES, r], NEEDED[r], -m))[part]
+            remote(held[0, r], held[m, r], r, span, 0, 1, m).wait_recv()
+            missing[m, r] -= 1
+            if not missing[m, r]:
+                here.add((m, r))
 
         def place(key, ref, at, a, b):
             if key not in made and source(a, b) in here:
@@ -215,8 +224,8 @@
                         if 1 <= step <= STEPS:
                             every[a, step - 1] = got[a * BLK : (a + 1) * BLK, c * BLK : (c + 1) * BLK]
 
-        for distance, r in FIRST_SENDS[lane]:
-            pass_on(0, r, distance)
+        for distance, r, part in FIRST_SENDS[lane]:
+            pass_on(0, r, part, distance)
         notes = []
         for k, m in enumerate(OTHERS):
             note = pltpu.make_async_remote_copy(
@@ -230,15 +239,15 @@
             note.start()
             notes.append(note)
         assemble()
-        for m, r in order[: last_relay + 1]:
-            arrive(m, r)
-            pass_on(m, r)
+        for item in order[: last_relay + 1]:
+            arrive(*item)
+            pass_on(*item)
         for note in notes:
             note.wait()
-        for m, r in order[last_relay + 1 :]:
+        for item in order[last_relay + 1 :]:
             assemble()
             multiply()
-            arrive(m, r)
+            arrive(*item)
         assemble()
         multiply()
         for copy in sent:
@@ -258,7 +267,7 @@
     rows, kept_count = result_cols.shape
     places_shape = pltpu.SMEM((ROWS, REACH + 1), jnp.int32)
     most_sent = max(
-        sum(len(hops(lane, m, r)) for m, r in ARRIVALS[lane] + ((0, 0), (0, 1))) for lane in range(LANES)
+        len(FIRST_SENDS[lane]) + sum(len(hops(lane, *item)) for item in ARRIVALS[lane]) for lane in range(LANES)
     )
 
     def kernel(*refs):
@@ -284,7 +293,7 @@
             pltpu.SMEM(upper_cols.shape, upper_cols.dtype),
             pltpu.SMEM(result_cols.shape, result_cols.dtype),
             pltpu.SemaphoreType.DMA((most_sent,)),
-            pltpu.SemaphoreType.DMA((len(OTHERS), ROWS)),
+            pltpu.SemaphoreType.DMA((len(OTHERS), ROWS, 2)),
             pltpu.SemaphoreType.DMA((len(OTHERS),)),
             pltpu.SemaphoreType.DMA((len(OTHERS),)),
             pltpu.SemaphoreType.DMA((3,)),

time: 33.1 us -> 31.2 us (0.943)
  the two profiles are of different devices: /device:TPU:8 before, /device:TPU:16 now
where the time goes in v5:
time: 31.2 us; the launch traced here: 31.1 us
  Pallas kernels  30.3 us (97%)
  local copies, waits for them, and re-layouts  0.8 us (3%)
    pallas_call x1, Pallas kernels, on_device(): pl.pallas_call(kernel, out_shape=jax.ShapeDtypeStruct((rows, kept_count,...  30.3 us
    unnamed x1, local copies, waits for them, and re-layouts  0.8 us

profile of v5, /device:TPU:16, one launch (start us, length us, event | category | flops | bytes accessed | tf_op | source)
XLA Modules:
  0.0 31.1 jit_solution(14041246087315496845)
XLA Ops:
  0.0 30.3 %shard_map.37 = bf16[2,8,128,128]{3,2,1,0:T(8,128)(2,1)S(1)} custom-call(bf16[2,6,128,128]{3,2,1,0:T(8,128)(2,1)} %refs_0_.1, s32[2,6]{1,0:T(2,128)} %refs_1_.1, s32[2,8]{1,0:T(2,128)} %refs_2_.1), custom_call_target="tpu_custom_call" | custom-call | flops 1200000000 | bytes 6000000 | tf_op jit(solution)/shard_map/pallas_call | solution.py:276
  30.3 0.8 %copy.5 = bf16[2,8,128,128]{3,2,1,0:T(8,128)(2,1)} copy(bf16[2,8,128,128]{3,2,1,0:T(8,128)(2,1)S(1)} %shard_map.37) | data formatting | bytes 1048576

commit v6 on v5

--- a/solution.py
+++ b/solution.py
@@ -23,56 +23,86 @@
     {1: 5, 2: 4, 3: 2, -1: 6, -2: 6, -3: 6, -4: 6},
     {1: 5, 2: 5, 3: 3, -1: 6, -2: 6, -3: 6},
 )
+PARTS = ((0, 3), (3, 6))
+HALF = BLK // 2
+PACKED = HALF + 16
+UNIT = 16
+UNITS = BLK // UNIT
 TREES = {
-    (0, 0): {3: 0, -3: -4, 2: 1, -2: -1, 1: 0, -1: -4, -4: 0},
-    (0, 1): {3: 0, 2: 3, -3: 1, 1: 0, -1: 3, -2: -3},
-    (1, 0): {-4: 0, 2: -1, 1: 0, -2: -3, 3: -1, -3: -4, -1: 0},
-    (1, 1): {-2: 2, 3: -1, 2: 1, -3: 1, 1: 0, -1: 0},
-    (2, 0): {2: -2, -3: -4, 3: -1, -4: 0, 1: -2, -2: -1, -1: 0},
-    (2, 1): {1: 0, 3: -1, -3: 1, -2: 1, 2: 3, -1: 0},
-    (3, 0): {3: -1, 1: -3, -4: 0, 2: -2, -3: 0, -1: 0, -2: -1},
-    (3, 1): {3: -1, -2: -3, 1: -3, -3: 0, 2: 3, -1: 0},
+    (0, 0, 0): {3: 0, -1: -4, -2: -3, -3: -4, -4: 0, 2: 1, 1: 0},
+    (0, 0, 1): {2: 0, -3: -4, -1: -4, -2: -3, -4: 0, 1: -3},
+    (0, 1, 0): {3: 0, -3: 1, 2: 3, -1: 3, -2: 2, 1: 0},
+    (0, 1, 1): {2: 1, 1: 0, -2: -3, -1: -3, -3: 1},
+    (1, 0, 0): {-1: 0, 3: 2, -3: -4, 1: 2, 2: -1, -4: 0, -2: 2},
+    (1, 0, 1): {-3: -4, -4: 0, 2: -1, 1: 2, -1: 0, -2: -3},
+    (1, 1, 0): {-3: 1, -1: 0, -2: -3, 2: 1, 1: 0, 3: -1},
+    (1, 1, 1): {1: 0, -2: -3, -1: 0, 2: 1, -3: 1},
+    (2, 0, 0): {-2: -1, 2: -2, -4: 0, -3: -4, 1: -2, -1: 0, 3: -1},
+    (2, 0, 1): {1: -3, 2: -1, -1: 0, -4: 0, -2: -1, -3: -4},
+    (2, 1, 0): {1: 0, 2: 3, -2: 1, -3: 1, -1: 0, 3: -1},
+    (2, 1, 1): {2: 1, -3: 1, -1: 0, 1: 0, -2: 1},
+    (3, 0, 0): {-4: 0, 1: -3, 2: 1, -2: -1, -1: 0, -3: 0, 3: -1},
+    (3, 0, 1): {-1: 0, 1: -3, -3: 0, 2: 1, -4: 0, -2: -1},
+    (3, 1, 0): {-2: -3, 2: 3, -1: 0, 3: -1, -3: 0, 1: -3},
+    (3, 1, 1): {-1: 0, -3: 0, -2: -3, 1: -3, 2: -1},
 }
 ARRIVALS = {
-    0: ((1, 1, 0), (4, 0, 0), (3, 1, 0), (1, 0, 0), (3, 0, 0), (4, 0, 1), (1, 1, 1), (3, 1, 1), (-3, 1, 0), (1, 0, 1), (3, 0, 1), (-1, 1, 0), (2, 0, 0), (-3, 0, 0), (2, 1, 0), (-1, 0, 0), (2, 0, 1), (2, 1, 1), (-1, 1, 1), (-2, 1, 0), (-1, 0, 1), (-2, 1, 1), (-2, 0, 0), (-2, 0, 1)),
-    1: ((-1, 0, 0), (1, 0, 0), (4, 0, 0), (-1, 1, 0), (1, 1, 0), (4, 0, 1), (-1, 0, 1), (-3, 0, 0), (1, 0, 1), (-1, 1, 1), (1, 1, 1), (3, 1, 0), (-3, 1, 0), (2, 1, 0), (2, 0, 0), (3, 0, 0), (2, 0, 1), (-3, 1, 1), (3, 1, 1), (3, 0, 1), (-2, 1, 0), (-2, 0, 0), (2, 1, 1), (-2, 0, 1), (-2, 1, 1)),
-    2: ((-1, 0, 0), (1, 0, 0), (4, 0, 0), (-1, 1, 0), (1, 1, 0), (4, 0, 1), (-1, 0, 1), (-3, 0, 0), (1, 0, 1), (-1, 1, 1), (1, 1, 1), (3, 1, 0), (-3, 1, 0), (-2, 0, 0), (-2, 1, 0), (3, 0, 0), (-2, 1, 1), (3, 1, 1), (-3, 1, 1), (3, 0, 1), (2, 0, 0), (-2, 0, 1), (2, 0, 1), (2, 1, 0), (2, 1, 1)),
-    3: ((-3, 1, 0), (-1, 1, 0), (4, 0, 0), (-3, 0, 0), (-1, 1, 1), (4, 0, 1), (-3, 1, 1), (3, 0, 0), (1, 1, 0), (1, 0, 0), (3, 1, 0), (-2, 1, 0), (3, 0, 1), (-2, 0, 0), (3, 1, 1), (1, 0, 1), (-2, 0, 1), (-2, 1, 1), (1, 1, 1), (-1, 0, 0), (2, 0, 0), (2, 1, 0), (-1, 0, 1), (2, 1, 1), (2, 0, 1)),
+    0: ((1, 0, 0), (3, 0, 1), (4, 0, 0), (1, 1, 0), (4, 0, 1), (3, 0, 0), (-1, 0, 1), (1, 1, 1), (3, 1, 1), (1, 0, 1), (3, 1, 0), (-1, 0, 0), (-3, 1, 0), (2, 0, 0), (2, 1, 0), (-2, 1, 1), (-1, 1, 1), (2, 0, 1), (-2, 0, 1), (2, 1, 1), (-1, 1, 0), (-3, 0, 0), (-2, 0, 0), (-2, 1, 0)),
+    1: ((-1, 1, 1), (4, 0, 1), (1, 0, 0), (-1, 0, 0), (4, 0, 0), (1, 1, 0), (-1, 1, 0), (1, 0, 1), (3, 1, 1), (-3, 0, 0), (3, 0, 0), (1, 1, 1), (-3, 1, 0), (2, 0, 1), (3, 0, 1), (3, 1, 0), (-2, 0, 1), (2, 1, 1), (-2, 1, 1), (-2, 1, 0), (-1, 0, 1), (2, 0, 0), (2, 1, 0), (-2, 0, 0)),
+    2: ((-1, 1, 1), (1, 0, 1), (4, 0, 0), (-1, 1, 0), (1, 1, 0), (4, 0, 1), (-2, 1, 1), (1, 1, 1), (3, 1, 1), (-2, 0, 1), (3, 0, 1), (1, 0, 0), (-3, 1, 0), (3, 1, 0), (-2, 0, 0), (3, 0, 0), (-2, 1, 0), (-1, 0, 0), (-3, 0, 0), (2, 1, 1), (2, 0, 0), (2, 1, 0), (-1, 0, 1), (2, 0, 1)),
+    3: ((-3, 0, 0), (-1, 1, 0), (4, 0, 0), (-3, 1, 0), (-1, 1, 1), (4, 0, 1), (-2, 1, 1), (3, 1, 0), (-2, 0, 0), (3, 0, 0), (1, 0, 0), (1, 1, 0), (1, 0, 1), (-2, 1, 0), (3, 0, 1), (3, 1, 1), (-2, 0, 1), (2, 1, 1), (2, 0, 0), (-1, 0, 0), (2, 0, 1), (1, 1, 1), (-1, 0, 1), (2, 1, 0)),
 }
 FIRST_SENDS = {
-    0: ((3, 1, 0), (3, 0, 0), (3, 1, 1), (1, 0, 0), (1, 1, 0), (1, 0, 1), (1, 1, 1), (-4, 0, 0), (-4, 0, 1)),
-    1: ((-4, 0, 0), (-4, 0, 1), (1, 0, 0), (1, 1, 0), (1, 0, 1), (1, 1, 1), (-1, 1, 0), (-1, 0, 0), (-1, 1, 1), (-1, 0, 1)),
-    2: ((-4, 0, 0), (-4, 0, 1), (1, 1, 0), (1, 1, 1), (-1, 0, 0), (-1, 1, 0), (-1, 0, 1), (-1, 1, 1)),
-    3: ((-4, 0, 0), (-4, 0, 1), (-3, 1, 0), (-3, 0, 0), (-3, 1, 1), (-3, 0, 1), (-1, 0, 0), (-1, 1, 0), (-1, 0, 1), (-1, 1, 1)),
+    0: ((3, 0, 0), (3, 1, 0), (2, 0, 1), (1, 1, 1), (-4, 0, 0), (1, 0, 0), (-4, 0, 1), (1, 1, 0)),
+    1: ((-1, 0, 0), (-1, 1, 0), (1, 1, 1), (-1, 1, 1), (-4, 0, 1), (-4, 0, 0), (1, 1, 0), (-1, 0, 1)),
+    2: ((1, 1, 0), (-4, 0, 0), (-1, 0, 0), (-1, 1, 0), (-1, 0, 1), (-4, 0, 1), (-1, 1, 1), (1, 1, 1)),
+    3: ((-1, 0, 1), (-3, 0, 1), (-4, 0, 0), (-1, 1, 0), (-1, 1, 1), (-4, 0, 1), (-1, 0, 0), (-3, 0, 0), (-3, 1, 1), (-3, 1, 0)),
 }
 LANES = 4
-FRONT = 3
-
-
-def size(tree, needed, node):
-    below = [size(tree, needed, n) for n, parent in tree.items() if parent == node]
-    return max(below + [needed.get(node, 0)])
-
-
-def parts(count):
-    return [(0, count)] if count <= FRONT else [(0, FRONT), (FRONT, count - FRONT)]
+
+
+def size(lane, r, part, node):
+    first, end = PARTS[part]
+    mine = max(min(NEEDED[r].get(node, 0), end) - first, 0)
+    below = [size(lane, r, part, n) for n, parent in TREES[lane, r, part].items() if parent == node]
+    return max(below + [mine])
 
 
 def hops(lane, distance, r, part):
-    tree = TREES[(lane + distance) % LANES, r]
-    found = []
-    for node, parent in tree.items():
-        spans = parts(size(tree, NEEDED[r], node))
-        if parent == -distance and part < len(spans):
-            found.append((node + distance, -node, spans[part]))
-    return found
+    tree = TREES[(lane + distance) % LANES, r, part]
+    return [(node + distance, -node) for node, parent in tree.items() if parent == -distance]
+
+
+def halves(shape):
+    return (lax.broadcasted_iota(jnp.int32, shape, axis) for axis in (0, 1))
+
+
+def packed(whole):
+    whole = whole.astype(jnp.float32)
+    upper, lower = whole[:HALF], pltpu.roll(whole[HALF:], HALF, axis=1)
+    i, j = halves((HALF, BLK))
+    middle = jnp.sum(jnp.where(i == j, lower, 0.0), axis=0, keepdims=True)
+    return (
+        jnp.where(i > j, lower, upper).astype(jnp.bfloat16),
+        jnp.broadcast_to(middle, (PACKED - HALF, BLK)).astype(jnp.bfloat16),
+    )
+
+
+def unpacked(rows, middle):
+    rows, middle = rows.astype(jnp.float32), middle.astype(jnp.float32)[:1]
+    turned = jnp.concatenate([rows, jnp.zeros_like(rows)], axis=0).T
+    i, j = halves((HALF, BLK))
+    upper = jnp.where(i <= j, rows, turned[:HALF])
+    lower = jnp.where(i > j, rows, jnp.where(i == j, middle, turned[:HALF]))
+    lower = jnp.where(j < HALF, turned[HALF:], pltpu.roll(lower, HALF, axis=1))
+    return jnp.concatenate([upper, lower], axis=0).astype(jnp.bfloat16)
 
 
 def band_kernel(device_total, block_total, vals_hbm, cols_hbm, kept_hbm, out, *scratch):
     held = {(m, r): scratch[i * ROWS + r] for i, m in enumerate((0, *OTHERS)) for r in range(ROWS)}
     places = dict(zip((0, *OTHERS), scratch[16:24]))
-    left, right, sums, every, vals, cols, kept = scratch[24:31]
-    send_sem, recv_sem, psend_sem, precv_sem, fetch_sem = scratch[31:]
+    left, right, sums, every, vals, cols, kept, middles = scratch[24:32]
+    send_sem, recv_sem, psend_sem, precv_sem, fetch_sem = scratch[32:]
     inner = lax.axis_size("col")
     me = lax.axis_index("row") * inner + lax.axis_index("col")
 
@@ -93,7 +123,7 @@
     zero = jnp.zeros((BLK, BLK), jnp.bfloat16)
     for m in (0, *OTHERS):
         for r in range(ROWS):
-            held[m, r][NONE] = zero
+            held[m, r][pl.ds(NONE * UNITS, UNITS)] = zero.reshape(UNITS, UNIT, BLK)
     fetches[0].wait()
     slots = []
     for r in range(ROWS):
@@ -110,7 +140,7 @@
                 for j in range(SLOTS - 1)
             ]
         )
-        places[0][r, 0] = SLOTS - 1
+        places[0][r, 0] = 0
         for o in range(1, REACH + 1):
             place = NONE
             for s in range(1, SLOTS):
@@ -119,30 +149,43 @@
     fetches[1].wait()
     for r in range(ROWS):
         for j in range(SLOTS - 1):
-            held[0, r][j] = vals[r, slots[r][j]]
-        held[0, r][SLOTS - 1] = vals[r, 0]
+            held[0, r][pl.ds(j * UNITS, UNITS)] = vals[r, slots[r][j]].reshape(UNITS, UNIT, BLK)
+        middle = vals[r, 0]
+        middle = (middle.astype(jnp.float32) + middle.T.astype(jnp.float32)).astype(jnp.bfloat16)
+        middles[r] = middle
+        rows, last = packed(middle)
+        held[0, r][pl.ds((SLOTS - 1) * UNITS, UNITS // 2)] = rows.reshape(UNITS // 2, UNIT, BLK)
+        held[0, r][(SLOTS - 1) * UNITS + UNITS // 2] = last
     fetches[2].wait()
 
     pl.semaphore_wait(barrier, 8)
 
-    def remote(source, target, r, span, send, distance, there):
+    def remote(lane, m, there, r, part, send, distance):
+        blocks = size((lane + m) % LANES, r, part, -there)
+        rows = blocks * BLK - (BLK - PACKED if PARTS[part][0] + blocks == SLOTS else 0)
+        span = pl.ds(PARTS[part][0] * UNITS, rows // UNIT)
         return pltpu.make_async_remote_copy(
-            src_ref=source.at[pl.ds(*span)],
-            dst_ref=target.at[pl.ds(*span)],
+            src_ref=held[m, r].at[span],
+            dst_ref=held[there, r].at[span],
             send_sem=send_sem.at[send],
-            recv_sem=recv_sem.at[OTHERS.index(there), r, 0 if span[0] == 0 else 1],
+            recv_sem=recv_sem.at[OTHERS.index(there), r, part],
             device_id=device(distance),
             device_id_type=pl.DeviceIdType.MESH,
         )
 
     def stored(row, offset):
         m, r = row // 2 - 3, row % 2
-        return held[m, r][places[m][r, offset]]
+        first = places[m][r, offset] * UNITS
+        return jnp.concatenate([held[m, r][first + k] for k in range(UNITS)], axis=0)
 
     def block(a, b):
         if a == b:
-            d = stored(a, 0)
-            return (d.astype(jnp.float32) + d.T.astype(jnp.float32)).astype(jnp.bfloat16)
+            m, r = a // 2 - 3, a % 2
+            if m == 0:
+                return middles[r]
+            first = (SLOTS - 1) * UNITS
+            rows = held[m, r][pl.ds(first, UNITS // 2)].reshape(HALF, BLK)
+            return unpacked(rows, held[m, r][first + UNITS // 2])
         if a < b:
             return stored(a, b - a)
         return stored(b, a - b).T
@@ -163,15 +206,14 @@
         missing = {item: sum(item == (m, r) for m, r, _ in order) for item in {(m, r) for m, r, _ in order}}
 
         def pass_on(m, r, part, only=None):
-            for distance, there, span in hops(lane, m, r, part):
+            for distance, there in hops(lane, m, r, part):
                 if only in (None, distance):
-                    copy = remote(held[m, r], held[there, r], r, span, len(sent), distance, there)
+                    copy = remote(lane, m, there, r, part, len(sent), distance)
                     copy.start()
                     sent.append(copy)
 
         def arrive(m, r, part):
-            span = parts(size(TREES[(lane + m) % LANES, r], NEEDED[r], -m))[part]
-            remote(held[0, r], held[m, r], r, span, 0, 1, m).wait_recv()
+            remote(lane, m, m, r, part, 0, 1).wait_recv()
             missing[m, r] -= 1
             if not missing[m, r]:
                 here.add((m, r))
@@ -283,7 +325,7 @@
         ],
         out_specs=pl.BlockSpec(memory_space=pltpu.VMEM),
         scratch_shapes=[
-            *[pltpu.VMEM((SLOTS + 1, BLK, BLK), jnp.bfloat16) for _ in range(ROWS * (1 + len(OTHERS)))],
+            *[pltpu.VMEM(((SLOTS + 1) * UNITS, UNIT, BLK), jnp.bfloat16) for _ in range(ROWS * (1 + len(OTHERS)))],
             *[places_shape for _ in range(1 + len(OTHERS))],
             pltpu.VMEM((ROWS * BLK, 2 * PAIRS * BLK), jnp.bfloat16),
             pltpu.VMEM((PAIRS, 2 * PAIRS * BLK, 2 * BLK), jnp.bfloat16),
@@ -292,6 +334,7 @@
             pltpu.VMEM(upper_vals.shape, upper_vals.dtype),
             pltpu.SMEM(upper_cols.shape, upper_cols.dtype),
             pltpu.SMEM(result_cols.shape, result_cols.dtype),
+            pltpu.VMEM((ROWS, BLK, BLK), jnp.bfloat16),
             pltpu.SemaphoreType.DMA((most_sent,)),
             pltpu.SemaphoreType.DMA((len(OTHERS), ROWS, 2)),
             pltpu.SemaphoreType.DMA((len(OTHERS),)),

time: 31.2 us -> 29.4 us (0.942)
  the two profiles are of different devices: /device:TPU:16 before, /device:TPU:8 now
where the time goes in v6:
time: 29.4 us; the launch traced here: 29.3 us
  Pallas kernels  28.5 us (97%)
  local copies, waits for them, and re-layouts  0.8 us (3%)
    pallas_call x1, Pallas kernels, on_device(): pl.pallas_call(kernel, out_shape=jax.ShapeDtypeStruct((rows, kept_count,...  28.5 us
    unnamed x1, local copies, waits for them, and re-layouts  0.8 us

profile of v6, /device:TPU:8, one launch (start us, length us, event | category | flops | bytes accessed | tf_op | source)
XLA Modules:
  0.0 29.3 jit_solution(8998064562854322644)
XLA Ops:
  0.0 28.5 %shard_map.37 = bf16[2,8,128,128]{3,2,1,0:T(8,128)(2,1)S(1)} custom-call(bf16[2,6,128,128]{3,2,1,0:T(8,128)(2,1)} %refs_0_.1, s32[2,6]{1,0:T(2,128)} %refs_1_.1, s32[2,8]{1,0:T(2,128)} %refs_2_.1), custom_call_target="tpu_custom_call" | custom-call | flops 1200000000 | bytes 6000000 | tf_op jit(solution)/shard_map/pallas_call | solution.py:318
  28.5 0.8 %copy.5 = bf16[2,8,128,128]{3,2,1,0:T(8,128)(2,1)} copy(bf16[2,8,128,128]{3,2,1,0:T(8,128)(2,1)S(1)} %shard_map.37) | data formatting | bytes 1048576

commit v7 on v6

--- a/solution.py
+++ b/solution.py
@@ -29,34 +29,34 @@
 UNIT = 16
 UNITS = BLK // UNIT
 TREES = {
-    (0, 0, 0): {3: 0, -1: -4, -2: -3, -3: -4, -4: 0, 2: 1, 1: 0},
-    (0, 0, 1): {2: 0, -3: -4, -1: -4, -2: -3, -4: 0, 1: -3},
-    (0, 1, 0): {3: 0, -3: 1, 2: 3, -1: 3, -2: 2, 1: 0},
-    (0, 1, 1): {2: 1, 1: 0, -2: -3, -1: -3, -3: 1},
-    (1, 0, 0): {-1: 0, 3: 2, -3: -4, 1: 2, 2: -1, -4: 0, -2: 2},
-    (1, 0, 1): {-3: -4, -4: 0, 2: -1, 1: 2, -1: 0, -2: -3},
-    (1, 1, 0): {-3: 1, -1: 0, -2: -3, 2: 1, 1: 0, 3: -1},
-    (1, 1, 1): {1: 0, -2: -3, -1: 0, 2: 1, -3: 1},
-    (2, 0, 0): {-2: -1, 2: -2, -4: 0, -3: -4, 1: -2, -1: 0, 3: -1},
-    (2, 0, 1): {1: -3, 2: -1, -1: 0, -4: 0, -2: -1, -3: -4},
-    (2, 1, 0): {1: 0, 2: 3, -2: 1, -3: 1, -1: 0, 3: -1},
-    (2, 1, 1): {2: 1, -3: 1, -1: 0, 1: 0, -2: 1},
-    (3, 0, 0): {-4: 0, 1: -3, 2: 1, -2: -1, -1: 0, -3: 0, 3: -1},
-    (3, 0, 1): {-1: 0, 1: -3, -3: 0, 2: 1, -4: 0, -2: -1},
-    (3, 1, 0): {-2: -3, 2: 3, -1: 0, 3: -1, -3: 0, 1: -3},
-    (3, 1, 1): {-1: 0, -3: 0, -2: -3, 1: -3, 2: -1},
+    (0, 0, 0): {-1: -4, 3: -1, 1: 0, -4: 0, -3: -4, -2: -3, 2: 1},
+    (0, 0, 1): {2: 3, -3: -4, 1: -3, -4: 0, -2: -3, 3: 0, -1: -4},
+    (0, 1, 0): {3: 0, -1: 3, 2: 3, -2: 2, 1: 0, -3: 1},
+    (0, 1, 1): {-3: 1, 1: 0, 3: 0, -1: 3, -2: -1, 2: 3},
+    (1, 0, 0): {-1: 0, 1: 2, 2: -1, -2: -3, 3: -1, -4: 0, -3: -4},
+    (1, 0, 1): {1: -3, -1: 0, 2: -1, -4: 0, -3: -4, -2: 2},
+    (1, 1, 0): {1: 0, -2: -3, 3: -1, -3: 1, 2: -1, -1: 0},
+    (1, 1, 1): {2: -1, -3: 0, 1: 0, -2: -3, -1: 0},
+    (2, 0, 0): {-2: 1, 1: 0, 2: -2, -4: 0, 3: -1, -3: -4, -1: 0},
+    (2, 0, 1): {1: 0, -1: 0, 2: -1, -2: -1, -3: -4, -4: 0},
+    (2, 1, 0): {3: -1, 1: 0, -3: 1, 2: 3, -2: -1, -1: 0},
+    (2, 1, 1): {-1: 0, 2: 1, -2: 1, 1: 0, -3: 1},
+    (3, 0, 0): {-2: -1, 3: -1, -4: 0, 2: 1, -3: 0, 1: -3, -1: 0},
+    (3, 0, 1): {2: 1, -2: -1, -3: 0, -1: 0, -4: 0, 1: -3},
+    (3, 1, 0): {3: -1, 2: 3, -1: 0, -3: 0, 1: -3, -2: -3},
+    (3, 1, 1): {3: -1, 1: -3, -3: 0, -1: 0, -2: -3, 2: 3},
 }
 ARRIVALS = {
-    0: ((1, 0, 0), (3, 0, 1), (4, 0, 0), (1, 1, 0), (4, 0, 1), (3, 0, 0), (-1, 0, 1), (1, 1, 1), (3, 1, 1), (1, 0, 1), (3, 1, 0), (-1, 0, 0), (-3, 1, 0), (2, 0, 0), (2, 1, 0), (-2, 1, 1), (-1, 1, 1), (2, 0, 1), (-2, 0, 1), (2, 1, 1), (-1, 1, 0), (-3, 0, 0), (-2, 0, 0), (-2, 1, 0)),
-    1: ((-1, 1, 1), (4, 0, 1), (1, 0, 0), (-1, 0, 0), (4, 0, 0), (1, 1, 0), (-1, 1, 0), (1, 0, 1), (3, 1, 1), (-3, 0, 0), (3, 0, 0), (1, 1, 1), (-3, 1, 0), (2, 0, 1), (3, 0, 1), (3, 1, 0), (-2, 0, 1), (2, 1, 1), (-2, 1, 1), (-2, 1, 0), (-1, 0, 1), (2, 0, 0), (2, 1, 0), (-2, 0, 0)),
-    2: ((-1, 1, 1), (1, 0, 1), (4, 0, 0), (-1, 1, 0), (1, 1, 0), (4, 0, 1), (-2, 1, 1), (1, 1, 1), (3, 1, 1), (-2, 0, 1), (3, 0, 1), (1, 0, 0), (-3, 1, 0), (3, 1, 0), (-2, 0, 0), (3, 0, 0), (-2, 1, 0), (-1, 0, 0), (-3, 0, 0), (2, 1, 1), (2, 0, 0), (2, 1, 0), (-1, 0, 1), (2, 0, 1)),
-    3: ((-3, 0, 0), (-1, 1, 0), (4, 0, 0), (-3, 1, 0), (-1, 1, 1), (4, 0, 1), (-2, 1, 1), (3, 1, 0), (-2, 0, 0), (3, 0, 0), (1, 0, 0), (1, 1, 0), (1, 0, 1), (-2, 1, 0), (3, 0, 1), (3, 1, 1), (-2, 0, 1), (2, 1, 1), (2, 0, 0), (-1, 0, 0), (2, 0, 1), (1, 1, 1), (-1, 0, 1), (2, 1, 0)),
+    0: ((1, 0, 0), (3, 0, 1), (4, 0, 0), (1, 0, 1), (3, 0, 0), (4, 0, 1), (3, 1, 1), (1, 1, 0), (-1, 0, 1), (-3, 0, 0), (3, 1, 0), (1, 1, 1), (-2, 0, 1), (-1, 0, 0), (2, 0, 1), (2, 0, 0), (-1, 1, 1), (-3, 1, 0), (2, 1, 0), (2, 1, 1), (-2, 1, 1), (-1, 1, 0), (-2, 1, 0), (-2, 0, 0)),
+    1: ((-1, 0, 0), (1, 0, 1), (4, 0, 0), (1, 1, 1), (-1, 1, 1), (1, 1, 0), (-1, 1, 0), (4, 0, 1), (1, 0, 0), (3, 0, 0), (3, 1, 1), (2, 0, 1), (3, 0, 1), (-3, 1, 0), (3, 1, 0), (2, 1, 1), (-2, 0, 1), (2, 0, 0), (-3, 0, 0), (-2, 1, 0), (2, 1, 0), (-1, 0, 1), (-2, 1, 1), (-2, 0, 0)),
+    2: ((-1, 1, 0), (1, 0, 1), (4, 0, 0), (-1, 1, 1), (1, 1, 0), (4, 0, 1), (1, 1, 1), (3, 1, 1), (3, 1, 0), (-2, 0, 0), (1, 0, 0), (3, 0, 0), (-3, 1, 0), (-2, 1, 0), (-3, 1, 1), (-2, 0, 1), (3, 0, 1), (-3, 0, 0), (-2, 1, 1), (2, 0, 0), (2, 1, 0), (-1, 0, 0), (-1, 0, 1), (2, 0, 1), (2, 1, 1)),
+    3: ((-3, 1, 0), (-1, 1, 0), (4, 0, 0), (-3, 0, 1), (-1, 0, 0), (4, 0, 1), (-3, 1, 1), (-1, 0, 1), (1, 1, 0), (-2, 0, 0), (-1, 1, 1), (3, 1, 0), (1, 0, 0), (3, 0, 0), (1, 1, 1), (-2, 0, 1), (3, 0, 1), (1, 0, 1), (3, 1, 1), (-3, 0, 0), (2, 1, 1), (-2, 1, 0), (2, 1, 0), (2, 0, 1), (-2, 1, 1), (2, 0, 0)),
 }
 FIRST_SENDS = {
-    0: ((3, 0, 0), (3, 1, 0), (2, 0, 1), (1, 1, 1), (-4, 0, 0), (1, 0, 0), (-4, 0, 1), (1, 1, 0)),
-    1: ((-1, 0, 0), (-1, 1, 0), (1, 1, 1), (-1, 1, 1), (-4, 0, 1), (-4, 0, 0), (1, 1, 0), (-1, 0, 1)),
-    2: ((1, 1, 0), (-4, 0, 0), (-1, 0, 0), (-1, 1, 0), (-1, 0, 1), (-4, 0, 1), (-1, 1, 1), (1, 1, 1)),
-    3: ((-1, 0, 1), (-3, 0, 1), (-4, 0, 0), (-1, 1, 0), (-1, 1, 1), (-4, 0, 1), (-1, 0, 0), (-3, 0, 0), (-3, 1, 1), (-3, 1, 0)),
+    0: ((3, 1, 0), (1, 0, 0), (-4, 0, 0), (1, 1, 1), (-4, 0, 1), (3, 0, 1), (1, 1, 0), (3, 1, 1)),
+    1: ((1, 1, 0), (-1, 0, 0), (-4, 0, 0), (-1, 0, 1), (-3, 1, 1), (-4, 0, 1), (1, 1, 1), (-1, 1, 0), (-1, 1, 1)),
+    2: ((1, 1, 0), (1, 0, 0), (1, 0, 1), (-4, 0, 0), (-1, 0, 1), (-1, 1, 1), (1, 1, 1), (-4, 0, 1), (-1, 1, 0), (-1, 0, 0)),
+    3: ((-3, 0, 1), (-1, 0, 1), (-4, 0, 0), (-1, 1, 0), (-4, 0, 1), (-3, 0, 0), (-3, 1, 1), (-1, 1, 1), (-3, 1, 0), (-1, 0, 0)),
 }
 LANES = 4
 

time: 29.4 us -> 29 us (0.986)
  the two profiles are of different devices: /device:TPU:8 before, /device:TPU:1 now
where the time goes in v7:
time: 29 us; the launch traced here: 28.9 us
  Pallas kernels  28.1 us (97%)
  local copies, waits for them, and re-layouts  0.8 us (3%)
    pallas_call x1, Pallas kernels, on_device(): pl.pallas_call(kernel, out_shape=jax.ShapeDtypeStruct((rows, kept_count,...  28.1 us
    unnamed x1, local copies, waits for them, and re-layouts  0.8 us

profile of v7, /device:TPU:1, one launch (start us, length us, event | category | flops | bytes accessed | tf_op | source)
XLA Modules:
  0.0 28.9 jit_solution(13619060971696201728)
XLA Ops:
  0.0 28.1 %shard_map.37 = bf16[2,8,128,128]{3,2,1,0:T(8,128)(2,1)S(1)} custom-call(bf16[2,6,128,128]{3,2,1,0:T(8,128)(2,1)} %refs_0_.1, s32[2,6]{1,0:T(2,128)} %refs_1_.1, s32[2,8]{1,0:T(2,128)} %refs_2_.1), custom_call_target="tpu_custom_call" | custom-call | flops 1200000000 | bytes 6000000 | tf_op jit(solution)/shard_map/pallas_call | solution.py:318
  28.1 0.8 %copy.5 = bf16[2,8,128,128]{3,2,1,0:T(8,128)(2,1)} copy(bf16[2,8,128,128]{3,2,1,0:T(8,128)(2,1)S(1)} %shard_map.37) | data formatting | bytes 1048576

commit v8 on v7

--- a/solution.py
+++ b/solution.py
@@ -29,34 +29,34 @@
 UNIT = 16
 UNITS = BLK // UNIT
 TREES = {
-    (0, 0, 0): {-1: -4, 3: -1, 1: 0, -4: 0, -3: -4, -2: -3, 2: 1},
-    (0, 0, 1): {2: 3, -3: -4, 1: -3, -4: 0, -2: -3, 3: 0, -1: -4},
-    (0, 1, 0): {3: 0, -1: 3, 2: 3, -2: 2, 1: 0, -3: 1},
-    (0, 1, 1): {-3: 1, 1: 0, 3: 0, -1: 3, -2: -1, 2: 3},
-    (1, 0, 0): {-1: 0, 1: 2, 2: -1, -2: -3, 3: -1, -4: 0, -3: -4},
-    (1, 0, 1): {1: -3, -1: 0, 2: -1, -4: 0, -3: -4, -2: 2},
-    (1, 1, 0): {1: 0, -2: -3, 3: -1, -3: 1, 2: -1, -1: 0},
-    (1, 1, 1): {2: -1, -3: 0, 1: 0, -2: -3, -1: 0},
-    (2, 0, 0): {-2: 1, 1: 0, 2: -2, -4: 0, 3: -1, -3: -4, -1: 0},
-    (2, 0, 1): {1: 0, -1: 0, 2: -1, -2: -1, -3: -4, -4: 0},
-    (2, 1, 0): {3: -1, 1: 0, -3: 1, 2: 3, -2: -1, -1: 0},
-    (2, 1, 1): {-1: 0, 2: 1, -2: 1, 1: 0, -3: 1},
-    (3, 0, 0): {-2: -1, 3: -1, -4: 0, 2: 1, -3: 0, 1: -3, -1: 0},
-    (3, 0, 1): {2: 1, -2: -1, -3: 0, -1: 0, -4: 0, 1: -3},
-    (3, 1, 0): {3: -1, 2: 3, -1: 0, -3: 0, 1: -3, -2: -3},
-    (3, 1, 1): {3: -1, 1: -3, -3: 0, -1: 0, -2: -3, 2: 3},
+    (0, 0, 0): {-2: -3, -1: -4, 2: 1, -4: 0, 1: 0, -3: -4, 3: 2},
+    (0, 0, 1): {-2: -3, 3: 0, 2: 3, 1: -3, -3: -4, -4: 0, -1: -4},
+    (0, 1, 0): {1: 0, -3: 1, -1: 3, -2: -3, 2: 3, 3: 0},
+    (0, 1, 1): {-2: -1, -1: 3, -3: 1, 2: 3, 3: 0, 1: 0},
+    (1, 0, 0): {-4: 0, -3: -4, -2: 2, -1: 0, 1: 2, 3: -1, 2: -1},
+    (1, 0, 1): {-4: 0, -1: 0, 1: 2, -2: 2, 2: -1, -3: -4},
+    (1, 1, 0): {-3: 1, 2: -1, -2: -3, 3: -1, -1: 0, 1: 0},
+    (1, 1, 1): {-3: 1, 1: 0, -2: -3, -1: 0, 2: -1},
+    (2, 0, 0): {2: -1, -2: 1, -1: 0, -4: 0, 1: 0, 3: -1, -3: -4},
+    (2, 0, 1): {-4: 0, -3: -4, -1: 0, 1: 0, 2: 1, -2: 1},
+    (2, 1, 0): {3: -1, -3: 1, -1: 0, 1: 0, -2: 1, 2: 3},
+    (2, 1, 1): {1: 0, 3: 0, 2: 3, -2: 1, -3: 1, -1: 0},
+    (3, 0, 0): {-4: 0, 1: -3, 3: -1, -3: 0, -1: 0, -2: -1, 2: 1},
+    (3, 0, 1): {-2: -1, 1: -3, 2: 1, -3: 0, -4: 0, -1: 0},
+    (3, 1, 0): {1: -3, -1: 0, 3: -1, -2: -3, 2: 3, -3: 0},
+    (3, 1, 1): {1: -3, -2: -3, 2: -1, -3: 0, -1: 0},
 }
 ARRIVALS = {
-    0: ((1, 0, 0), (3, 0, 1), (4, 0, 0), (1, 0, 1), (3, 0, 0), (4, 0, 1), (3, 1, 1), (1, 1, 0), (-1, 0, 1), (-3, 0, 0), (3, 1, 0), (1, 1, 1), (-2, 0, 1), (-1, 0, 0), (2, 0, 1), (2, 0, 0), (-1, 1, 1), (-3, 1, 0), (2, 1, 0), (2, 1, 1), (-2, 1, 1), (-1, 1, 0), (-2, 1, 0), (-2, 0, 0)),
-    1: ((-1, 0, 0), (1, 0, 1), (4, 0, 0), (1, 1, 1), (-1, 1, 1), (1, 1, 0), (-1, 1, 0), (4, 0, 1), (1, 0, 0), (3, 0, 0), (3, 1, 1), (2, 0, 1), (3, 0, 1), (-3, 1, 0), (3, 1, 0), (2, 1, 1), (-2, 0, 1), (2, 0, 0), (-3, 0, 0), (-2, 1, 0), (2, 1, 0), (-1, 0, 1), (-2, 1, 1), (-2, 0, 0)),
-    2: ((-1, 1, 0), (1, 0, 1), (4, 0, 0), (-1, 1, 1), (1, 1, 0), (4, 0, 1), (1, 1, 1), (3, 1, 1), (3, 1, 0), (-2, 0, 0), (1, 0, 0), (3, 0, 0), (-3, 1, 0), (-2, 1, 0), (-3, 1, 1), (-2, 0, 1), (3, 0, 1), (-3, 0, 0), (-2, 1, 1), (2, 0, 0), (2, 1, 0), (-1, 0, 0), (-1, 0, 1), (2, 0, 1), (2, 1, 1)),
-    3: ((-3, 1, 0), (-1, 1, 0), (4, 0, 0), (-3, 0, 1), (-1, 0, 0), (4, 0, 1), (-3, 1, 1), (-1, 0, 1), (1, 1, 0), (-2, 0, 0), (-1, 1, 1), (3, 1, 0), (1, 0, 0), (3, 0, 0), (1, 1, 1), (-2, 0, 1), (3, 0, 1), (1, 0, 1), (3, 1, 1), (-3, 0, 0), (2, 1, 1), (-2, 1, 0), (2, 1, 0), (2, 0, 1), (-2, 1, 1), (2, 0, 0)),
+    0: ((1, 0, 0), (4, 0, 0), (3, 0, 0), (1, 0, 1), (3, 0, 1), (4, 0, 1), (1, 1, 0), (3, 1, 0), (-3, 0, 0), (-1, 0, 0), (1, 1, 1), (3, 1, 1), (-1, 0, 1), (-2, 1, 1), (2, 1, 0), (-2, 0, 1), (-3, 1, 0), (2, 0, 1), (-2, 1, 0), (-1, 1, 0), (-2, 0, 0), (2, 1, 1), (-1, 1, 1), (2, 0, 0)),
+    1: ((-1, 1, 0), (4, 0, 0), (1, 1, 0), (-1, 0, 0), (4, 0, 1), (1, 0, 1), (-3, 1, 1), (-1, 1, 1), (3, 1, 0), (1, 0, 0), (-3, 1, 0), (3, 0, 0), (1, 1, 1), (3, 0, 1), (3, 1, 1), (2, 0, 0), (2, 1, 0), (-3, 0, 0), (-2, 0, 0), (2, 0, 1), (-2, 1, 1), (-2, 1, 0), (-1, 0, 1), (2, 1, 1), (-2, 0, 1)),
+    2: ((-1, 1, 1), (1, 1, 0), (4, 0, 1), (-1, 1, 0), (1, 0, 0), (4, 0, 0), (1, 0, 1), (3, 0, 0), (3, 1, 1), (-3, 1, 0), (1, 1, 1), (-2, 0, 1), (3, 0, 1), (-2, 0, 0), (-3, 0, 0), (3, 1, 0), (-2, 1, 0), (-2, 1, 1), (2, 1, 0), (2, 0, 0), (-1, 0, 0), (2, 0, 1), (2, 1, 1), (-1, 0, 1)),
+    3: ((-3, 0, 1), (-1, 1, 0), (4, 0, 0), (-3, 1, 0), (-1, 0, 1), (4, 0, 1), (-3, 1, 1), (-1, 1, 1), (3, 1, 0), (-2, 0, 0), (-1, 0, 0), (1, 0, 0), (1, 1, 0), (3, 0, 1), (1, 1, 1), (-2, 0, 1), (1, 0, 1), (3, 0, 0), (3, 1, 1), (2, 0, 0), (-2, 1, 0), (2, 1, 1), (-3, 0, 0), (-2, 1, 1), (2, 0, 1), (2, 1, 0)),
 }
 FIRST_SENDS = {
-    0: ((3, 1, 0), (1, 0, 0), (-4, 0, 0), (1, 1, 1), (-4, 0, 1), (3, 0, 1), (1, 1, 0), (3, 1, 1)),
-    1: ((1, 1, 0), (-1, 0, 0), (-4, 0, 0), (-1, 0, 1), (-3, 1, 1), (-4, 0, 1), (1, 1, 1), (-1, 1, 0), (-1, 1, 1)),
-    2: ((1, 1, 0), (1, 0, 0), (1, 0, 1), (-4, 0, 0), (-1, 0, 1), (-1, 1, 1), (1, 1, 1), (-4, 0, 1), (-1, 1, 0), (-1, 0, 0)),
-    3: ((-3, 0, 1), (-1, 0, 1), (-4, 0, 0), (-1, 1, 0), (-4, 0, 1), (-3, 0, 0), (-3, 1, 1), (-1, 1, 1), (-3, 1, 0), (-1, 0, 0)),
+    0: ((1, 1, 0), (3, 0, 1), (-4, 0, 0), (1, 0, 0), (3, 1, 0), (-4, 0, 1), (3, 1, 1), (1, 1, 1)),
+    1: ((-4, 0, 0), (-4, 0, 1), (-1, 0, 0), (-1, 0, 1), (-1, 1, 0), (1, 1, 1), (-1, 1, 1), (1, 1, 0)),
+    2: ((-1, 1, 0), (-4, 0, 1), (1, 1, 0), (-1, 0, 1), (1, 0, 1), (1, 1, 1), (3, 1, 1), (-1, 0, 0), (-4, 0, 0), (1, 0, 0), (-1, 1, 1)),
+    3: ((-4, 0, 0), (-1, 1, 0), (-3, 0, 0), (-1, 0, 0), (-3, 0, 1), (-4, 0, 1), (-1, 0, 1), (-3, 1, 0), (-3, 1, 1), (-1, 1, 1)),
 }
 LANES = 4
 

time: 29 us -> 28.6 us (0.986)
  the two profiles are of different devices: /device:TPU:1 before, /device:TPU:8 now
where the time goes in v8:
time: 28.6 us; the launch traced here: 28.4 us
  Pallas kernels  27.6 us (97%)
  local copies, waits for them, and re-layouts  0.8 us (3%)
    pallas_call x1, Pallas kernels, on_device(): pl.pallas_call(kernel, out_shape=jax.ShapeDtypeStruct((rows, kept_count,...  27.6 us
    unnamed x1, local copies, waits for them, and re-layouts  0.8 us

profile of v8, /device:TPU:8, one launch (start us, length us, event | category | flops | bytes accessed | tf_op | source)
XLA Modules:
  0.0 28.4 jit_solution(9233108693116527607)
XLA Ops:
  0.0 27.6 %shard_map.37 = bf16[2,8,128,128]{3,2,1,0:T(8,128)(2,1)S(1)} custom-call(bf16[2,6,128,128]{3,2,1,0:T(8,128)(2,1)} %refs_0_.1, s32[2,6]{1,0:T(2,128)} %refs_1_.1, s32[2,8]{1,0:T(2,128)} %refs_2_.1), custom_call_target="tpu_custom_call" | custom-call | flops 1200000000 | bytes 6000000 | tf_op jit(solution)/shard_map/pallas_call | solution.py:318
  27.6 0.8 %copy.5 = bf16[2,8,128,128]{3,2,1,0:T(8,128)(2,1)} copy(bf16[2,8,128,128]{3,2,1,0:T(8,128)(2,1)S(1)} %shard_map.37) | data formatting | bytes 1048576

commit v9 on v8

--- a/solution.py
+++ b/solution.py
@@ -292,16 +292,16 @@
             arrive(*item)
         assemble()
         multiply()
+        for a in range(ROWS):
+            for t in range(kept.shape[1]):
+                step = lax.rem(kept[a, t] - (me * ROWS + a) + block_total, block_total)
+                out[a, t] = every[a, jnp.clip(step - 1, 0, STEPS - 1)]
         for copy in sent:
             copy.wait_send()
 
     lane_here = lax.rem(me, LANES)
     for lane in range(LANES):
         pl.when(lane_here == lane)(functools.partial(traffic, lane))
-    for a in range(ROWS):
-        for t in range(kept.shape[1]):
-            step = lax.rem(kept[a, t] - (me * ROWS + a) + block_total, block_total)
-            out[a, t] = every[a, jnp.clip(step - 1, 0, STEPS - 1)]
 
 
 def on_device(upper_vals, upper_cols, result_cols):

time: 28.6 us -> 28.5 us (level)
  no operation moved by 1% of the time
where the time goes in v9:
time: 28.5 us; the launch traced here: 28.3 us
  Pallas kernels  27.5 us (96%)
  local copies, waits for them, and re-layouts  0.8 us (3%)
    pallas_call x1, Pallas kernels, on_device(): pl.pallas_call(kernel, out_shape=jax.ShapeDtypeStruct((rows, kept_count,...  27.5 us
    unnamed x1, local copies, waits for them, and re-layouts  0.8 us

profile of v9, /device:TPU:8, one launch (start us, length us, event | category | flops | bytes accessed | tf_op | source)
XLA Modules:
  0.0 28.3 jit_solution(6027282965279098484)
XLA Ops:
  0.0 27.5 %shard_map.37 = bf16[2,8,128,128]{3,2,1,0:T(8,128)(2,1)S(1)} custom-call(bf16[2,6,128,128]{3,2,1,0:T(8,128)(2,1)} %refs_0_.1, s32[2,6]{1,0:T(2,128)} %refs_1_.1, s32[2,8]{1,0:T(2,128)} %refs_2_.1), custom_call_target="tpu_custom_call" | custom-call | flops 1200000000 | bytes 6000000 | tf_op jit(solution)/shard_map/pallas_call | solution.py:318
  27.5 0.8 %copy.5 = bf16[2,8,128,128]{3,2,1,0:T(8,128)(2,1)} copy(bf16[2,8,128,128]{3,2,1,0:T(8,128)(2,1)S(1)} %shard_map.37) | data formatting | bytes 1048576
